TPU v7x, 128 devices: a whole 4x4x4 slice. The times are simulated.
128 devices in a mesh: pair: 8 (over z, core), ri: 16 (over y, x).
Axes of the slice: x: 4, y: 4, z: 4, core: 2. Of those that a mesh axis runs over, the one named last changes fastest.
Arguments:
- integrals: bfloat16 [128, 5, 144, 128, 128], P('pair', None, 'ri'), may hold values from -0.23632812 to 0.23632812
- lam_index: int32 [128, 5], P('pair'), may hold values from 0 to 127, as said below
- tile_count: int32 [128], P('pair'), may hold values from 1 to 5
- screen: int32 [128, 5], P('pair'), may hold values 0 or 1
- coefficients: bfloat16 [128, 16384], P(None, ('pair', 'ri')), may hold values from -0.52734375 to 0.52734375
- metric: bfloat16 [144, 144], replicated, may hold values from -0.5 to 0.5
Outputs:
- exchange: float32 [16384, 2048], P(('pair', 'ri'))
Inputs may be any that keep to these rules, and one draw needn't show every extreme that they name: `lam_index`: slot 0 of block b names b itself; the partners of one block are distinct and lie ahead of it, cyclically, within 128 blocks.
All inputs are finite; a program needn't handle non-finite values. No bound on the sum of `screen` on one device may be relied on, other than what follows from the above.
Results may differ from a plain program's by a relative error of at most 0.0022.
Values may be sent and summed in bfloat16 or wider, within the bound.
No kernel may reach another device: no remote copies, remote signals or barrier semaphores. Data moves between devices by JAX's collectives and lax.ppermute only.
A program may use at most 256 MiB of HBM per device.

v0:
```python
import functools

import jax
import jax.numpy as jnp
from jax import lax
from jax.experimental import pallas as pl
from jax.experimental.pallas import tpu as pltpu
from jax.sharding import PartitionSpec as P

MIB = 1024 * 1024
NT = (((1,), (1,)), ((), ()))
SIDE = 4
HALVES = 2
ON_VMEM = pl.BlockSpec(memory_space=pltpu.VMEM)
ON_SMEM = pl.BlockSpec(memory_space=pltpu.SMEM)
ANYWHERE = pl.BlockSpec(memory_space=pl.ANY)


class Chunk:
    def __init__(self, x_first, steps, hops, handed):
        self.x_first, self.steps, self.hops, self.handed = x_first, steps, hops, handed
        self.held = steps + [steps[n] for n, _ in hops]

    def arrivals(self):
        return [tuple(-d % SIDE for d in self.held[n]) for n in self.handed]


CHUNKS = (
    Chunk(False, [(0, 0), (1, 0), (1, 1), (1, 2), (1, 3)], [(2, 1), (3, 2), (4, 3)], [1, 5, 6, 7]),
    Chunk(True, [(0, 1), (0, 2), (2, 0), (2, 1), (2, 2)], [(3, 2)], [0, 5]),
)


class Table:
    def __init__(self, blocks, slots):
        self.blocks, self.slots = blocks, slots
        self.count = 0
        self.slot = self.count + blocks
        self.core = self.slot + blocks * slots
        self.name = self.core + blocks * slots
        self.x = self.name + blocks * slots
        self.y = self.x + 1
        self.size = self.y + 1


def prepare_kernel(at, place, lam, tile_count, screen, table):
    core = place[0]
    table[at.x] = place[1]
    table[at.y] = place[2]

    def one(b, _):
        count = jnp.int32(0)
        for s in range(at.slots):
            name = lam[b, s]
            to = b * at.slots + count
            table[at.slot + to] = s
            table[at.core + to] = ((name >> 4) ^ core) & 1
            table[at.name + to] = ((name >> 5) << 4) | (name & 15)
            keep = jnp.logical_and(s < tile_count[b], screen[b, s] > 0)
            count = count + keep.astype(jnp.int32)
        table[at.count + b] = count
        return 0

    lax.fori_loop(0, at.blocks, one, 0)


def prepare(at, place, lam, tile_count, screen):
    return pl.pallas_call(
        functools.partial(prepare_kernel, at),
        in_specs=[ON_SMEM] * 4,
        out_specs=ON_SMEM,
        out_shape=jax.ShapeDtypeStruct((at.size,), jnp.int32),
        name="prepare",
    )(place, lam, tile_count, screen)


def gather(coefficients):
    copies = jnp.broadcast_to(coefficients[None], (lax.axis_size(("z", "y", "x")),) + coefficients.shape)
    same = lax.all_to_all(copies, ("z", "y", "x"), 0, 0, tiled=True)
    return same, lax.ppermute(same, "core", [(0, 1), (1, 0)])


def fit_kernel(at, table, same, other, integrals, out, tiles, picked, total, done):
    slots = at.slots
    _, _, size = same.shape
    ri, own_q, rows, _ = out.shape
    share = rows // HALVES
    steps = at.blocks // HALVES

    def copy(block, j):
        slot = table[at.slot + block * slots + j]
        return pltpu.make_async_copy(integrals.at[block, slot], tiles.at[block, j], done.at[block, j])

    def kept(block, act):
        for j in range(slots):
            @pl.when(j < table[at.count + block])
            def _():
                act(copy(block, j))

    def begin(step, _):
        for half in range(HALVES):
            kept(step + half * steps, lambda c: c.start())
        return 0

    lax.fori_loop(0, steps, begin, 0)

    def one(step, _):
        for half in range(HALVES):
            block = step + half * steps
            count = table[at.count + block]
            kept(block, lambda c: c.wait())

            @pl.when(count == 0)
            def _():
                total[half] = jnp.zeros(total.shape[1:], total.dtype)

            for c in range(1, slots + 1):
                @pl.when(count == c)
                def _():
                    for j in range(c):
                        n = block * slots + j
                        name = table[at.name + n]
                        tile = jnp.where(table[at.core + n] == 0, same[name], other[name])
                        picked[half, :, j * size:(j + 1) * size] = tile
                    wide = [tiles[block, j].reshape(own_q * size, size) for j in range(c)]
                    wide = jnp.concatenate(wide, axis=1) if c > 1 else wide[0]
                    total[half] = lax.dot_general(
                        picked[half, :, :c * size], wide, NT, preferred_element_type=jnp.float32
                    )

        for q in range(own_q):
            parts = [
                total[half, :, q * size:(q + 1) * size].reshape(ri, share, size) for half in range(HALVES)
            ]
            out[:, q, :, pl.ds(pl.multiple_of(step * size, size), size)] = (
                jnp.concatenate(parts, axis=1).astype(out.dtype)
            )
        return 0

    lax.fori_loop(0, steps, one, 0)


def fit(at, table, integrals, same, other):
    blocks, slots, own_q, size, _ = integrals.shape
    occupied = same.shape[1]
    ri = SIDE * SIDE
    share = occupied // ri
    return pl.pallas_call(
        functools.partial(fit_kernel, at),
        in_specs=[ON_SMEM, ON_VMEM, ON_VMEM, ANYWHERE],
        out_specs=ON_VMEM,
        scratch_shapes=[
            pltpu.VMEM((blocks, slots, own_q, size, size), jnp.bfloat16),
            pltpu.VMEM((HALVES, occupied, slots * size), jnp.bfloat16),
            pltpu.VMEM((HALVES, occupied, own_q * size), jnp.float32),
            pltpu.SemaphoreType.DMA((blocks, slots)),
        ],
        out_shape=jax.ShapeDtypeStruct((ri, own_q, HALVES * share, blocks // HALVES * size), jnp.bfloat16),
        compiler_params=pltpu.CompilerParams(vmem_limit_bytes=40 * MIB),
        cost_estimate=pl.CostEstimate(flops=3 * 10 ** 9, bytes_accessed=20 * 10 ** 6, transcendentals=0),
        name="fit",
    )(table, same, other, integrals)


def factor_kernel(metric, fitted, factors, turned, wide):
    ri, own_q, rows, half_cols = fitted.shape
    share = rows // HALVES
    n_q = metric.shape[0]
    lanes, tile = wide.shape[1], wide.shape[3]
    chunk = lanes * tile

    def one(c, _):
        base = pl.multiple_of(c * chunk, chunk)
        for k in range(own_q):
            x = fitted[:, k, :, pl.ds(base, chunk)].astype(jnp.float32)
            for r in range(ri):
                to = (r * own_q + k) * share
                for h in range(HALVES):
                    for t in range(lanes):
                        wide[h, t, to:to + share, :] = x[r, h * share:(h + 1) * share, t * tile:(t + 1) * tile]
        for h in range(HALVES):
            start = pl.multiple_of(base + h * half_cols, chunk)
            parts = []
            for o in range(share):
                x = jnp.concatenate(
                    [wide[h, t, pl.ds(o, n_q, stride=share), :] for t in range(lanes)], axis=1
                ).astype(jnp.bfloat16)
                parts.append(jnp.dot(metric[...], x, preferred_element_type=jnp.float32).astype(jnp.bfloat16))
            whole = jnp.concatenate(parts, axis=0)
            factors[:, pl.ds(start, chunk)] = whole
            turned[pl.ds(start, chunk), :] = whole.T
        return 0

    lax.fori_loop(0, half_cols // chunk, one, 0)


def factor(metric, fitted):
    ri, own_q, rows, half_cols = fitted.shape
    cols = HALVES * half_cols
    depth = own_q * ri * rows // HALVES
    return pl.pallas_call(
        factor_kernel,
        in_specs=[ON_VMEM] * 2,
        out_specs=[ON_VMEM] * 2,
        out_shape=[
            jax.ShapeDtypeStruct((depth, cols), jnp.bfloat16),
            jax.ShapeDtypeStruct((cols, depth), jnp.bfloat16),
        ],
        scratch_shapes=[pltpu.VMEM((HALVES, 2, depth, cols // ri), jnp.float32)],
        compiler_params=pltpu.CompilerParams(vmem_limit_bytes=20 * MIB),
        cost_estimate=pl.CostEstimate(flops=2 * 10 ** 9, bytes_accessed=10 * 10 ** 6, transcendentals=0),
        name="factor",
    )(metric, fitted)


def panel_kernel(at, chunk, table, factors, turned, *rest):
    outs, panels = rest[-1 - SIDE:-1], rest[-1]
    _, size, _ = panels.shape
    line = SIDE * size

    def row(y, _):
        for dy in sorted({dy for dy, _ in chunk.steps}):
            wanted = [dx for to, dx in chunk.steps if to == dy]
            side = 2 if wanted == [0] else SIDE
            for low in range(0, SIDE, side):
                rows = turned[pl.ds(pl.multiple_of(y * line + low * size, side * size), side * size), :]
                start = pl.multiple_of(lax.rem(y + dy, SIDE) * line + low * size, side * size)
                value = jnp.dot(
                    rows, factors[:, pl.ds(start, side * size)], preferred_element_type=jnp.float32
                ).astype(jnp.bfloat16)
                for n in range(side):
                    for dx in wanted:
                        to = chunk.steps.index((dy, dx)) * size
                        col = (n + dx) % side * size
                        x = low + n
                        panels[y * SIDE + x, :, to:to + size] = value[n * size:(n + 1) * size, col:col + size]
        return 0

    lax.fori_loop(0, SIDE, row, 0)
    for k, out in enumerate(outs):
        to = lax.rem(table[at.x if chunk.x_first else at.y] + k, SIDE)
        for j in range(SIDE):
            out[j] = panels[j * SIDE + to if chunk.x_first else to * SIDE + j]


def panel_columns(at, chunk, weight, table, factors, turned, *after):
    cols, depth = turned.shape
    size = cols // (SIDE * SIDE)
    span = len(chunk.steps) * size
    return pl.pallas_call(
        functools.partial(panel_kernel, at, chunk),
        in_specs=[ON_SMEM, ON_VMEM, ON_VMEM] + [ANYWHERE] * len(after),
        out_specs=[ON_VMEM] * SIDE,
        out_shape=[jax.ShapeDtypeStruct((SIDE, size, span), jnp.bfloat16)] * SIDE,
        scratch_shapes=[pltpu.VMEM((SIDE * SIDE, size, span), jnp.bfloat16)],
        compiler_params=pltpu.CompilerParams(vmem_limit_bytes=12 * MIB),
        cost_estimate=pl.CostEstimate(
            flops=weight * 4 * 10 ** 9, bytes_accessed=15 * 10 ** 6, transcendentals=0
        ),
        name="panel_columns",
    )(table, factors, turned, *after)


def first_sum_kernel(at, chunk, table, *rest):
    ins, outs = rest[:SIDE], rest[-SIDE:]
    size = outs[0].shape[0]
    own = len(chunk.steps) * size
    mine = table[at.y if chunk.x_first else at.x]

    def total(panel, start, stop):
        value = ins[0][panel, :, start:stop].astype(jnp.float32)
        for part in ins[1:]:
            value = value + part[panel, :, start:stop].astype(jnp.float32)
        return value

    for k, out in enumerate(outs):
        to = mine + k
        out[:, :own] = total(lax.rem(to, SIDE), 0, own).astype(out.dtype)
        for n, (position, back) in enumerate(chunk.hops):
            start = position * size
            value = total(lax.rem(to + SIDE - back, SIDE), start, start + size)
            out[:, own + n * size:own + (n + 1) * size] = value.astype(out.dtype)


def first_sum(at, chunk, table, parts):
    size = parts[0].shape[-2]
    shape = (size, len(chunk.held) * size)
    return pl.pallas_call(
        functools.partial(first_sum_kernel, at, chunk),
        in_specs=[ON_SMEM] + [ON_VMEM] * SIDE,
        out_specs=[ON_VMEM] * SIDE,
        out_shape=[jax.ShapeDtypeStruct(shape, jnp.bfloat16 if n else jnp.float32) for n in range(SIDE)],
        compiler_params=pltpu.CompilerParams(vmem_limit_bytes=16 * MIB),
        name="first_sum",
    )(table, *parts)


def second_sum_kernel(chunk, *refs):
    parts, own, handed = refs[:SIDE], refs[SIDE], refs[SIDE + 1]
    size, span = own.shape
    for n in range(len(chunk.held)):
        total = parts[0][:, n * size:(n + 1) * size]
        for part in parts[1:]:
            total = total + part[:, n * size:(n + 1) * size].astype(jnp.float32)
        if n * size < span:
            own[:, n * size:(n + 1) * size] = total
        if n in chunk.handed:
            handed[chunk.handed.index(n)] = total.T.astype(handed.dtype)


def second_sum(chunk, parts):
    size = parts[0].shape[0]
    return pl.pallas_call(
        functools.partial(second_sum_kernel, chunk),
        in_specs=[ON_VMEM] * SIDE,
        out_specs=[ON_VMEM] * 2,
        out_shape=[
            jax.ShapeDtypeStruct((size, len(chunk.steps) * size), jnp.float32),
            jax.ShapeDtypeStruct((len(chunk.handed), size, size), jnp.bfloat16),
        ],
        compiler_params=pltpu.CompilerParams(vmem_limit_bytes=16 * MIB),
        name="second_sum",
    )(*parts)


def place_kernel(at, table, *rest):
    owns, mirrors, out = rest[:len(CHUNKS)], rest[len(CHUNKS):-1], rest[-1]
    size = out.shape[0]

    def put(step, value):
        y = lax.rem(table[at.y] + step[0], SIDE)
        x = lax.rem(table[at.x] + step[1], SIDE)
        out[:, pl.ds(pl.multiple_of((y * SIDE + x) * size, size), size)] = value.astype(out.dtype)

    for chunk, own, mirror in zip(CHUNKS, owns, mirrors):
        for n, step in enumerate(chunk.steps):
            put(step, own[:, n * size:(n + 1) * size])
        for n, step in enumerate(chunk.arrivals()):
            put(step, mirror[n])


def place_blocks(at, table, owns, mirrors):
    size = owns[0].shape[0]
    return pl.pallas_call(
        functools.partial(place_kernel, at),
        in_specs=[ON_SMEM] + [ON_VMEM] * (len(owns) + len(mirrors)),
        out_specs=ON_VMEM,
        out_shape=jax.ShapeDtypeStruct((size, SIDE * SIDE * size), jnp.float32),
        compiler_params=pltpu.CompilerParams(vmem_limit_bytes=16 * MIB),
        name="place_blocks",
    )(table, *owns, *mirrors)


def along(axis, k):
    return functools.partial(lax.ppermute, axis_name=axis, perm=[(i, (i + k) % SIDE) for i in range(SIDE)])


def body(integrals, lam_index, tile_count, screen, coefficients, metric):
    at = Table(*integrals.shape[:2])
    place = jnp.stack([lax.axis_index(name).astype(jnp.int32) for name in ("core", "x", "y")])
    table = prepare(at, place, lam_index, tile_count, screen)
    same, other = gather(coefficients)
    mine = fit(at, table, integrals, same, other)
    fitted = lax.all_to_all(mine, ("y", "x"), 0, 0, tiled=True)
    factors, turned = factor(metric, fitted)

    def send(parts, axis):
        return [parts[0]] + [along(axis, k)(parts[k]) for k in range(1, SIDE)]

    owns, mirrors, after = [], [], []
    for chunk in CHUNKS:
        first, second = ("x", "y") if chunk.x_first else ("y", "x")
        panels = panel_columns(at, chunk, 20 if after else 1, table, factors, turned, *after)
        after = [panels[0]]
        sums = first_sum(at, chunk, table, send(panels, first))
        own, handed = second_sum(chunk, send(sums, second))
        owns.append(own)
        mirrors.append(along(first, 1)(handed))
    return place_blocks(at, table, owns, mirrors)


def solution(mesh):
    pair, ri = ("z", "core"), ("y", "x")
    cores = 2
    devices = mesh.devices.reshape(mesh.shape["pair"] // cores, cores, SIDE, SIDE)
    named = jax.sharding.Mesh(devices, pair + ri)
    placed = (
        P(pair, None, ri, None, None),
        P(pair, None),
        P(pair),
        P(pair, None),
        P(None, pair + ri),
        P(),
    )
    return jax.shard_map(
        body, mesh=named, in_specs=placed, out_specs=P(pair + ri, None), check_vma=False
    )
```

profile of v0, /device:TPU:0, one launch (start us, length us, event | category | flops | bytes accessed | tf_op | source)
XLA Modules:
  0.0 194.1 jit_solution(16419289409914787670)
XLA Ops:
  0.0 1.3 broadcast_in_dim.2
  1.3 41.3 %all_to_all.10.same = bf16[64,128,128]{2,1,0:T(8,128)(2,1)S(1)} all-to-all(bf16[64,128,128]{2,1,0:T(8,128)(2,1)S(1)} %broadcast_in_dim.2), channel_id=1, replica_groups=mesh['z'=4,'core'=2,'y'=4,'x'=4] {'z','y','x'}, dimensions={0} | all-to-all | bytes 4194304 | tf_op jit(solution)/shard_map/all_to_all | solution.py:79
  44.5 2.1 %prepare.1.table = s32[258]{0:T(512)} custom-call(s32[3]{0:T(128)} %pad_add_fusion.place, s32[16,5]{1,0:T(8,128)} %copy.7.lam, s32[16]{0:T(128)} %tile_count.1, s32[16,5]{1,0:T(8,128)} %copy.8.screen), custom_call_target="tpu_custom_call" | custom-call | tf_op jit(solution)/shard_map/prepare/pallas_call | solution.py:68
  47.5 11.4 %fit.1 = bf16[16,9,16,1024]{3,2,1,0:T(8,128)(2,1)S(1)} custom-call(s32[258]{0:T(512)S(1)} %copy-done, bf16[64,128,128]{2,1,0:T(8,128)(2,1)S(1)} %all_to_all.10.same, bf16[64,128,128]{2,1,0:T(8,128)(2,1)} %collective-permute-done.other, bf16[16,5,9,128,128]{4,3,2,1,0:T(8,128)(2,1)} %integrals.1), custom_call_target="tpu_custom_call" | custom-call | flops 3000000000 | bytes 20000000 | tf_op jit(solution)/shard_map/fit/pallas_call | solution.py:148
  58.9 59.5 %all_to_all.11.fitted = bf16[16,9,16,1024]{3,2,1,0:T(8,128)(2,1)S(1)} all-to-all(bf16[16,9,16,1024]{3,2,1,0:T(8,128)(2,1)S(1)} %fit.1), channel_id=1, replica_groups=mesh['z'=4,'core'=2,'y'=4,'x'=4] {'y','x'}, dimensions={0} | all-to-all | bytes 9437184 | tf_op jit(solution)/shard_map/all_to_all | solution.py:364
  118.4 3.4 %factor.1 = (bf16[1152,2048]{1,0:T(8,128)(2,1)S(1)}, bf16[2048,1152]{1,0:T(8,128)(2,1)S(1)}) custom-call(bf16[144,144]{1,0:T(8,128)(2,1)S(1)} %copy-done.1, bf16[16,9,16,1024]{3,2,1,0:T(8,128)(2,1)S(1)} %all_to_all.11.fitted), custom_call_target="tpu_custom_call" | custom-call | flops 2000000000 | bytes 10000000 | tf_op jit(solution)/shard_map/factor/pallas_call | solution.py:201
  121.8 5.7 %panel_columns.2 = (bf16[4,128,640]{2,1,0:T(8,128)(2,1)S(1)}, bf16[4,128,640]{2,1,0:T(8,128)(2,1)S(1)}, bf16[4,128,640]{2,1,0:T(8,128)(2,1)S(1)}, bf16[4,128,640]{2,1,0:T(8,128)(2,1)S(1)}) custom-call(s32[258]{0:T(512)S(1)} %copy-done, bf16[1152,2048]{1,0:T(8,128)(2,1)S(1)} %get-tuple-element.27.factors, bf16[2048,1152]{1,0:T(8,128)(2,1)S(1)} %get-tuple-element.28.turned), custom_call_target="tpu_custom_call" | custom-call | flops 4000000000 | bytes 15000000 | tf_op jit(solution)/shard_map/panel_columns/pallas_call | solution.py:250
  127.5 2.3 %collective-permute-start.2 = (bf16[4,128,640]{2,1,0:T(8,128)(2,1)S(1)}, bf16[4,128,640]{2,1,0:T(8,128)(2,1)S(1)}, u32[]{:S(2)}, u32[]{:S(2)}) collective-permute-start(bf16[4,128,640]{2,1,0:T(8,128)(2,1)S(1)} %get-tuple-element.31), channel_id=1, source_target_pairs={{0,8},{4,12},{8,0},{12,4},{1,9},{5,13},{9,1},{13,5},{2,10},{6,14},... | collective-permute-start | bytes 1966088 | tf_op jit(solution)/shard_map/ppermute | solution.py:368
  129.8 1.2 collective-permute-start.3
  131.0 6.9 %panel_columns.3 = (bf16[4,128,640]{2,1,0:T(8,128)(2,1)S(1)}, bf16[4,128,640]{2,1,0:T(8,128)(2,1)S(1)}, bf16[4,128,640]{2,1,0:T(8,128)(2,1)S(1)}, bf16[4,128,640]{2,1,0:T(8,128)(2,1)S(1)}) custom-call(s32[258]{0:T(512)S(1)} %copy-done, bf16[1152,2048]{1,0:T(8,128)(2,1)S(1)} %get-tuple-element.27.factors, bf16[2048,1152]{1,0:T(8,128)(2,1)S(1)} %get-tuple-element.28.turned, ...), custom_call_target="tpu_custom_call" | custom-call | flops 80000000000 | bytes 15000000 | tf_op jit(solution)/shard_map/panel_columns/pallas_call | solution.py:250
  138.5 2.1 %collective-permute-start.8 = (bf16[4,128,640]{2,1,0:T(8,128)(2,1)S(1)}, bf16[4,128,640]{2,1,0:T(8,128)(2,1)S(1)}, u32[]{:S(2)}, u32[]{:S(2)}) collective-permute-start(bf16[4,128,640]{2,1,0:T(8,128)(2,1)S(1)} %get-tuple-element.40), channel_id=1, source_target_pairs={{0,2},{1,3},{2,0},{3,1},{4,6},{5,7},{6,4},{7,5},{8,10},{9,11},{10,... | collective-permute-start | bytes 1966088 | tf_op jit(solution)/shard_map/ppermute | solution.py:368
  140.6 17.2 %collective-permute-done.1.rest_1_ = bf16[4,128,640]{2,1,0:T(8,128)(2,1)S(1)} collective-permute-done((bf16[4,128,640]{2,1,0:T(8,128)(2,1)S(1)}, bf16[4,128,640]{2,1,0:T(8,128)(2,1)S(1)}, u32[]{:S(2)}, u32[]{:S(2)}) %collective-permute-start.1) | collective-permute-done | bytes 655392 | tf_op jit(solution)/shard_map/ppermute | solution.py:368
  158.7 1.1 first_sum.2
  159.7 1.2 collective-permute-start.4
  160.9 1.0 collective-permute-start.5
  161.9 4.7 %collective-permute-done.7.rest_1_ = bf16[4,128,640]{2,1,0:T(8,128)(2,1)S(1)} collective-permute-done((bf16[4,128,640]{2,1,0:T(8,128)(2,1)S(1)}, bf16[4,128,640]{2,1,0:T(8,128)(2,1)S(1)}, u32[]{:S(2)}, u32[]{:S(2)}) %collective-permute-start.7) | collective-permute-done | bytes 655392 | tf_op jit(solution)/shard_map/ppermute | solution.py:368
  166.6 3.8 %collective-permute-done.8.rest_2_ = bf16[4,128,640]{2,1,0:T(8,128)(2,1)S(1)} collective-permute-done((bf16[4,128,640]{2,1,0:T(8,128)(2,1)S(1)}, bf16[4,128,640]{2,1,0:T(8,128)(2,1)S(1)}, u32[]{:S(2)}, u32[]{:S(2)}) %collective-permute-start.8) | collective-permute-done | bytes 655392 | tf_op jit(solution)/shard_map/ppermute | solution.py:368
  170.4 3.4 %collective-permute-done.9.rest_3_ = bf16[4,128,640]{2,1,0:T(8,128)(2,1)S(1)} collective-permute-done((bf16[4,128,640]{2,1,0:T(8,128)(2,1)S(1)}, bf16[4,128,640]{2,1,0:T(8,128)(2,1)S(1)}, u32[]{:S(2)}, u32[]{:S(2)}) %collective-permute-start.9) | collective-permute-done | bytes 655392 | tf_op jit(solution)/shard_map/ppermute | solution.py:368
  174.8 3.5 %collective-permute-start.11 = (bf16[128,768]{1,0:T(8,128)(2,1)S(1)}, bf16[128,768]{1,0:T(8,128)(2,1)S(1)}, u32[]{:S(2)}, u32[]{:S(2)}) collective-permute-start(bf16[128,768]{1,0:T(8,128)(2,1)S(1)} %get-tuple-element.44), channel_id=1, source_target_pairs={{0,8},{4,12},{8,0},{12,4},{1,9},{5,13},{9,1},{13,5},{2,10},{6,14},... | collective-permute-start | bytes 589832 | tf_op jit(solution)/shard_map/ppermute | solution.py:368
  179.9 1.4 collective-permute-start.13
  181.7 3.1 %collective-permute-done.11.refs_2_ = bf16[128,768]{1,0:T(8,128)(2,1)S(1)} collective-permute-done((bf16[128,768]{1,0:T(8,128)(2,1)S(1)}, bf16[128,768]{1,0:T(8,128)(2,1)S(1)}, u32[]{:S(2)}, u32[]{:S(2)}) %collective-permute-start.11) | collective-permute-done | bytes 196640 | tf_op jit(solution)/shard_map/ppermute | solution.py:368
  184.8 1.9 collective-permute-done.12.refs_3_
  187.0 5.5 %collective-permute-done.14.rest_3_ = bf16[2,128,128]{2,1,0:T(8,128)(2,1)S(1)} collective-permute-done((bf16[2,128,128]{2,1,0:T(8,128)(2,1)S(1)}, bf16[2,128,128]{2,1,0:T(8,128)(2,1)S(1)}, u32[]{:S(2)}, u32[]{:S(2)}) %collective-permute-start.14) | collective-permute-done | bytes 65568 | tf_op jit(solution)/shard_map/ppermute | solution.py:378
  192.5 1.6 place_blocks.1
  (30 shorter events, 7.6 us)
Async XLA Ops:
  0.0 42.5 %copy-start.2 = (s32[16,5]{0,1:T(8,128)S(1)}, s32[16,5]{0,1:T(8,128)}, u32[]{:S(2)}) copy-start(s32[16,5]{0,1:T(8,128)} %param.7) | copy-start | bytes 964
  0.0 43.2 %copy-start.3 = (s32[16,5]{0,1:T(8,128)S(1)}, s32[16,5]{0,1:T(8,128)}, u32[]{:S(2)}) copy-start(s32[16,5]{0,1:T(8,128)} %param.9) | copy-start | bytes 964
  42.5 4.3 %collective-permute-start = (bf16[64,128,128]{2,1,0:T(8,128)(2,1)S(1)}, bf16[64,128,128]{2,1,0:T(8,128)(2,1)}, u32[]{:S(2)}, u32[]{:S(2)}) collective-permute-start(bf16[64,128,128]{2,1,0:T(8,128)(2,1)S(1)} %all_to_all.10.same), channel_id=1, source_target_pairs={{0,16},{16,0},{1,17},{17,1},{2,18},{18,2},{3,19},{19,3},{4,20},{20... | collective-permute-start | bytes 6291464 | tf_op jit(solution)/shard_map/ppermute | solution.py:80
  46.8 0.6 copy-start
  58.9 59.5 %copy-start.1 = (bf16[144,144]{1,0:T(8,128)(2,1)S(1)}, bf16[144,144]{1,0:T(8,128)(2,1)}, u32[]{:S(2)}) copy-start(bf16[144,144]{1,0:T(8,128)(2,1)} %metric.1) | copy-start | bytes 124420
  127.4 30.4 %collective-permute-start.1 = (bf16[4,128,640]{2,1,0:T(8,128)(2,1)S(1)}, bf16[4,128,640]{2,1,0:T(8,128)(2,1)S(1)}, u32[]{:S(2)}, u32[]{:S(2)}) collective-permute-start(bf16[4,128,640]{2,1,0:T(8,128)(2,1)S(1)} %get-tuple-element.30), channel_id=1, source_target_pairs={{0,4},{4,8},{8,12},{12,0},{1,5},{5,9},{9,13},{13,1},{2,6},{6,10},{... | collective-permute-start | bytes 1966088 | tf_op jit(solution)/shard_map/ppermute | solution.py:368
  127.5 31.2 %collective-permute-start.2 = (bf16[4,128,640]{2,1,0:T(8,128)(2,1)S(1)}, bf16[4,128,640]{2,1,0:T(8,128)(2,1)S(1)}, u32[]{:S(2)}, u32[]{:S(2)}) collective-permute-start(bf16[4,128,640]{2,1,0:T(8,128)(2,1)S(1)} %get-tuple-element.31), channel_id=1, source_target_pairs={{0,8},{4,12},{8,0},{12,4},{1,9},{5,13},{9,1},{13,5},{2,10},{6,14},... | collective-permute-start | bytes 1966088 | tf_op jit(solution)/shard_map/ppermute | solution.py:368
  129.8 28.9 %collective-permute-start.3 = (bf16[4,128,640]{2,1,0:T(8,128)(2,1)S(1)}, bf16[4,128,640]{2,1,0:T(8,128)(2,1)S(1)}, u32[]{:S(2)}, u32[]{:S(2)}) collective-permute-start(bf16[4,128,640]{2,1,0:T(8,128)(2,1)S(1)} %get-tuple-element.32), channel_id=1, source_target_pairs={{0,12},{4,0},{8,4},{12,8},{1,13},{5,1},{9,5},{13,9},{2,14},{6,2},{... | collective-permute-start | bytes 1966088 | tf_op jit(solution)/shard_map/ppermute | solution.py:368
  137.9 28.7 %collective-permute-start.7 = (bf16[4,128,640]{2,1,0:T(8,128)(2,1)S(1)}, bf16[4,128,640]{2,1,0:T(8,128)(2,1)S(1)}, u32[]{:S(2)}, u32[]{:S(2)}) collective-permute-start(bf16[4,128,640]{2,1,0:T(8,128)(2,1)S(1)} %get-tuple-element.39), channel_id=1, source_target_pairs={{0,1},{1,2},{2,3},{3,0},{4,5},{5,6},{6,7},{7,4},{8,9},{9,10},{10,1... | collective-permute-start | bytes 1966088 | tf_op jit(solution)/shard_map/ppermute | solution.py:368
  138.5 31.9 %collective-permute-start.8 = (bf16[4,128,640]{2,1,0:T(8,128)(2,1)S(1)}, bf16[4,128,640]{2,1,0:T(8,128)(2,1)S(1)}, u32[]{:S(2)}, u32[]{:S(2)}) collective-permute-start(bf16[4,128,640]{2,1,0:T(8,128)(2,1)S(1)} %get-tuple-element.40), channel_id=1, source_target_pairs={{0,2},{1,3},{2,0},{3,1},{4,6},{5,7},{6,4},{7,5},{8,10},{9,11},{10,... | collective-permute-start | bytes 1966088 | tf_op jit(solution)/shard_map/ppermute | solution.py:368
  157.8 16.0 %collective-permute-start.9 = (bf16[4,128,640]{2,1,0:T(8,128)(2,1)S(1)}, bf16[4,128,640]{2,1,0:T(8,128)(2,1)S(1)}, u32[]{:S(2)}, u32[]{:S(2)}) collective-permute-start(bf16[4,128,640]{2,1,0:T(8,128)(2,1)S(1)} %get-tuple-element.41), channel_id=1, source_target_pairs={{0,3},{1,0},{2,1},{3,2},{4,7},{5,4},{6,5},{7,6},{8,11},{9,8},{10,9... | collective-permute-start | bytes 1966088 | tf_op jit(solution)/shard_map/ppermute | solution.py:368
  159.7 19.2 %collective-permute-start.4 = (bf16[128,1024]{1,0:T(8,128)(2,1)S(1)}, bf16[128,1024]{1,0:T(8,128)(2,1)S(1)}, u32[]{:S(2)}, u32[]{:S(2)}) collective-permute-start(bf16[128,1024]{1,0:T(8,128)(2,1)S(1)} %get-tuple-element.34), channel_id=1, source_target_pairs={{0,1},{1,2},{2,3},{3,0},{4,5},{5,6},{6,7},{7,4},{8,9},{9,10},{10,1... | collective-permute-start | bytes 786440 | tf_op jit(solution)/shard_map/ppermute | solution.py:368
  160.9 18.7 %collective-permute-start.5 = (bf16[128,1024]{1,0:T(8,128)(2,1)S(1)}, bf16[128,1024]{1,0:T(8,128)(2,1)S(1)}, u32[]{:S(2)}, u32[]{:S(2)}) collective-permute-start(bf16[128,1024]{1,0:T(8,128)(2,1)S(1)} %get-tuple-element.35), channel_id=1, source_target_pairs={{0,2},{1,3},{2,0},{3,1},{4,6},{5,7},{6,4},{7,5},{8,10},{9,11},{10,... | collective-permute-start | bytes 786440 | tf_op jit(solution)/shard_map/ppermute | solution.py:368
  166.6 13.0 %collective-permute-start.6 = (bf16[128,1024]{1,0:T(8,128)(2,1)S(1)}, bf16[128,1024]{1,0:T(8,128)(2,1)S(1)}, u32[]{:S(2)}, u32[]{:S(2)}) collective-permute-start(bf16[128,1024]{1,0:T(8,128)(2,1)S(1)} %get-tuple-element.36), channel_id=1, source_target_pairs={{0,3},{1,0},{2,1},{3,2},{4,7},{5,4},{6,5},{7,6},{8,11},{9,8},{10,9... | collective-permute-start | bytes 786440 | tf_op jit(solution)/shard_map/ppermute | solution.py:368
  174.7 6.9 %collective-permute-start.10 = (bf16[128,768]{1,0:T(8,128)(2,1)S(1)}, bf16[128,768]{1,0:T(8,128)(2,1)S(1)}, u32[]{:S(2)}, u32[]{:S(2)}) collective-permute-start(bf16[128,768]{1,0:T(8,128)(2,1)S(1)} %get-tuple-element.43), channel_id=1, source_target_pairs={{0,4},{4,8},{8,12},{12,0},{1,5},{5,9},{9,13},{13,1},{2,6},{6,10},{... | collective-permute-start | bytes 589832 | tf_op jit(solution)/shard_map/ppermute | solution.py:368
  174.8 10.0 %collective-permute-start.11 = (bf16[128,768]{1,0:T(8,128)(2,1)S(1)}, bf16[128,768]{1,0:T(8,128)(2,1)S(1)}, u32[]{:S(2)}, u32[]{:S(2)}) collective-permute-start(bf16[128,768]{1,0:T(8,128)(2,1)S(1)} %get-tuple-element.44), channel_id=1, source_target_pairs={{0,8},{4,12},{8,0},{12,4},{1,9},{5,13},{9,1},{13,5},{2,10},{6,14},... | collective-permute-start | bytes 589832 | tf_op jit(solution)/shard_map/ppermute | solution.py:368
  179.0 7.8 %collective-permute-start.12 = (bf16[128,768]{1,0:T(8,128)(2,1)S(1)}, bf16[128,768]{1,0:T(8,128)(2,1)S(1)}, u32[]{:S(2)}, u32[]{:S(2)}) collective-permute-start(bf16[128,768]{1,0:T(8,128)(2,1)S(1)} %get-tuple-element.45), channel_id=1, source_target_pairs={{0,12},{4,0},{8,4},{12,8},{1,13},{5,1},{9,5},{13,9},{2,14},{6,2},{... | collective-permute-start | bytes 589832 | tf_op jit(solution)/shard_map/ppermute | solution.py:368
  179.9 12.6 %collective-permute-start.13 = (bf16[4,128,128]{2,1,0:T(8,128)(2,1)S(1)}, bf16[4,128,128]{2,1,0:T(8,128)(2,1)S(1)}, u32[]{:S(2)}, u32[]{:S(2)}) collective-permute-start(bf16[4,128,128]{2,1,0:T(8,128)(2,1)S(1)} %get-tuple-element.47), channel_id=1, source_target_pairs={{0,4},{4,8},{8,12},{12,0},{1,5},{5,9},{9,13},{13,1},{2,6},{6,10},{... | collective-permute-start | bytes 393224 | tf_op jit(solution)/shard_map/ppermute | solution.py:378
  186.9 5.5 %collective-permute-start.14 = (bf16[2,128,128]{2,1,0:T(8,128)(2,1)S(1)}, bf16[2,128,128]{2,1,0:T(8,128)(2,1)S(1)}, u32[]{:S(2)}, u32[]{:S(2)}) collective-permute-start(bf16[2,128,128]{2,1,0:T(8,128)(2,1)S(1)} %get-tuple-element.48), channel_id=1, source_target_pairs={{0,1},{1,2},{2,3},{3,0},{4,5},{5,6},{6,7},{7,4},{8,9},{9,10},{10,1... | collective-permute-start | bytes 196616 | tf_op jit(solution)/shard_map/ppermute | solution.py:378
where the time goes:
time: 197 us; the launch traced here: 194 us
  blocking collectives  101 us (51%)
  waiting for transfers between devices  40.8 us (21%)
  Pallas kernels  33.5 us (17%)
  starting transfers between devices  15.1 us (8%)
  local copies, waits for them, and re-layouts  3.27 us (2%)
    all_to_all x1, blocking collectives, body(): fitted = lax.all_to_all(mine, ('y', 'x'), 0, 0, tiled=True)  59.5 us
    all_to_all x1, blocking collectives, gather(): same = lax.all_to_all(copies, ('z', 'y', 'x'), 0, 0, tiled=True)  41.3 us
    ppermute x12, waiting for transfers between devices, send(): return [parts[0]] + [along(axis, k)(parts[k]) for k in range(1, SIDE)]  35.1 us
    ppermute x12, starting transfers between devices, send(): return [parts[0]] + [along(axis, k)(parts[k]) for k in range(1, SIDE)]  13.6 us
    pallas_call x2, Pallas kernels, panel_columns(): pl.pallas_call(functools.partial(panel_kernel, at, chunk), in_specs=[ON_S...  12.6 us
    pallas_call x1, Pallas kernels, fit(): pl.pallas_call(functools.partial(fit_kernel, at), in_specs=[ON_SMEM, ON_V...  11.4 us
    ppermute x2, waiting for transfers between devices, body(): mirrors.append(along(first, 1)(handed))  5.47 us
  transfers between devices with their start and end apart: 15, of which 10 were waited for; matrix products, arithmetic and copies ran while one was open for 1% of the time, Pallas kernels for 6%

commit v1 on v0

--- a/solution.py
+++ b/solution.py
@@ -213,52 +213,56 @@
     )(metric, fitted)
 
 
-def panel_kernel(at, chunk, table, factors, turned, *rest):
-    outs, panels = rest[-1 - SIDE:-1], rest[-1]
-    _, size, _ = panels.shape
+def panel_kernel(at, table, factors, turned, *rest):
+    outs, panels = rest[:-1], rest[-1]
+    size = panels.shape[1]
     line = SIDE * size
-
-    def row(y, _):
-        for dy in sorted({dy for dy, _ in chunk.steps}):
-            wanted = [dx for to, dx in chunk.steps if to == dy]
-            side = 2 if wanted == [0] else SIDE
-            for low in range(0, SIDE, side):
-                rows = turned[pl.ds(pl.multiple_of(y * line + low * size, side * size), side * size), :]
-                start = pl.multiple_of(lax.rem(y + dy, SIDE) * line + low * size, side * size)
-                value = jnp.dot(
-                    rows, factors[:, pl.ds(start, side * size)], preferred_element_type=jnp.float32
-                ).astype(jnp.bfloat16)
-                for n in range(side):
-                    for dx in wanted:
-                        to = chunk.steps.index((dy, dx)) * size
-                        col = (n + dx) % side * size
-                        x = low + n
-                        panels[y * SIDE + x, :, to:to + size] = value[n * size:(n + 1) * size, col:col + size]
-        return 0
-
-    lax.fori_loop(0, SIDE, row, 0)
-    for k, out in enumerate(outs):
-        to = lax.rem(table[at.x if chunk.x_first else at.y] + k, SIDE)
-        for j in range(SIDE):
-            out[j] = panels[j * SIDE + to if chunk.x_first else to * SIDE + j]
-
-
-def panel_columns(at, chunk, weight, table, factors, turned, *after):
+    for k in range(SIDE):
+        y = lax.rem(table[at.y] + k, SIDE)
+        rows = turned[pl.ds(pl.multiple_of(y * line, line), line), :]
+        for dy in sorted({dy for chunk in CHUNKS for dy, _ in chunk.steps}):
+            start = pl.multiple_of(lax.rem(y + dy, SIDE) * line, line)
+            value = jnp.dot(
+                rows, factors[:, pl.ds(start, line)], preferred_element_type=jnp.float32
+            ).astype(jnp.bfloat16)
+            for n, chunk in enumerate(CHUNKS):
+                for position, step in enumerate(chunk.steps):
+                    if step[0] != dy:
+                        continue
+                    to = position * size
+                    for x in range(SIDE):
+                        col = (x + step[1]) % SIDE * size
+                        block = value[x * size:(x + 1) * size, col:col + size]
+                        if chunk.x_first:
+                            panels[y * SIDE + x, :, to:to + size] = block
+                        else:
+                            outs[n * SIDE + k][x, :, to:to + size] = block
+    for n, chunk in enumerate(CHUNKS):
+        if chunk.x_first:
+            for k in range(SIDE):
+                x = lax.rem(table[at.x] + k, SIDE)
+                for y in range(SIDE):
+                    outs[n * SIDE + k][y] = panels[y * SIDE + x]
+
+
+def panel_columns(at, table, factors, turned):
     cols, depth = turned.shape
     size = cols // (SIDE * SIDE)
-    span = len(chunk.steps) * size
-    return pl.pallas_call(
-        functools.partial(panel_kernel, at, chunk),
-        in_specs=[ON_SMEM, ON_VMEM, ON_VMEM] + [ANYWHERE] * len(after),
-        out_specs=[ON_VMEM] * SIDE,
-        out_shape=[jax.ShapeDtypeStruct((SIDE, size, span), jnp.bfloat16)] * SIDE,
-        scratch_shapes=[pltpu.VMEM((SIDE * SIDE, size, span), jnp.bfloat16)],
-        compiler_params=pltpu.CompilerParams(vmem_limit_bytes=12 * MIB),
-        cost_estimate=pl.CostEstimate(
-            flops=weight * 4 * 10 ** 9, bytes_accessed=15 * 10 ** 6, transcendentals=0
-        ),
+    widest = max(len(chunk.steps) for chunk in CHUNKS if chunk.x_first) * size
+    return pl.pallas_call(
+        functools.partial(panel_kernel, at),
+        in_specs=[ON_SMEM, ON_VMEM, ON_VMEM],
+        out_specs=[ON_VMEM] * (len(CHUNKS) * SIDE),
+        out_shape=[
+            jax.ShapeDtypeStruct((SIDE, size, len(chunk.steps) * size), jnp.bfloat16)
+            for chunk in CHUNKS
+            for _ in range(SIDE)
+        ],
+        scratch_shapes=[pltpu.VMEM((SIDE * SIDE, size, widest), jnp.bfloat16)],
+        compiler_params=pltpu.CompilerParams(vmem_limit_bytes=16 * MIB),
+        cost_estimate=pl.CostEstimate(flops=8 * 10 ** 9, bytes_accessed=15 * 10 ** 6, transcendentals=0),
         name="panel_columns",
-    )(table, factors, turned, *after)
+    )(table, factors, turned)
 
 
 def first_sum_kernel(at, chunk, table, *rest):
@@ -365,14 +369,13 @@
     factors, turned = factor(metric, fitted)
 
     def send(parts, axis):
-        return [parts[0]] + [along(axis, k)(parts[k]) for k in range(1, SIDE)]
-
-    owns, mirrors, after = [], [], []
-    for chunk in CHUNKS:
+        return [parts[0]] + [along(axis, k)(parts[k]) for k in (2, 1, 3)]
+
+    panels = panel_columns(at, table, factors, turned)
+    owns, mirrors = [], []
+    for n, chunk in enumerate(CHUNKS):
         first, second = ("x", "y") if chunk.x_first else ("y", "x")
-        panels = panel_columns(at, chunk, 20 if after else 1, table, factors, turned, *after)
-        after = [panels[0]]
-        sums = first_sum(at, chunk, table, send(panels, first))
+        sums = first_sum(at, chunk, table, send(panels[n * SIDE:(n + 1) * SIDE], first))
         own, handed = second_sum(chunk, send(sums, second))
         owns.append(own)
         mirrors.append(along(first, 1)(handed))

time: 197 us -> 189 us (0.959); the launches traced: 194 us -> 188 us
  Pallas kernels: 33.5 us -> 29.4 us
  waiting for transfers between devices: 40.8 us -> 38.6 us
    pallas_call x2 -> x1, Pallas kernels: 12.6 us -> 9.22 us  [panel_columns(): pl.pallas_call(functools.partial(panel_kernel, at), in_specs=[ON_SMEM, ON...]
    ppermute x12, waiting for transfers between devices: 35.1 us -> 33.1 us  [send(): return [parts[0]] + [along(axis, k)(parts[k]) for k in (2, 1, 3)]]
  transfers between devices with their start and end apart: 15 -> 15, of which waited for: 10 -> 7; matrix products, arithmetic and copies ran while one was open for 1% -> 1% of each run, Pallas kernels for 6% -> 2%
where the time goes in v1:
time: 189 us; the launch traced here: 188 us
  blocking collectives  102 us (54%)
  waiting for transfers between devices  38.6 us (20%)
  Pallas kernels  29.4 us (16%)
  starting transfers between devices  14.2 us (8%)
  local copies, waits for them, and re-layouts  3.3 us (2%)
    all_to_all x1, blocking collectives, body(): fitted = lax.all_to_all(mine, ('y', 'x'), 0, 0, tiled=True)  60.7 us
    all_to_all x1, blocking collectives, gather(): same = lax.all_to_all(copies, ('z', 'y', 'x'), 0, 0, tiled=True)  41.3 us
    ppermute x12, waiting for transfers between devices, send(): return [parts[0]] + [along(axis, k)(parts[k]) for k in (2, 1, 3)]  33.1 us
    ppermute x12, starting transfers between devices, send(): return [parts[0]] + [along(axis, k)(parts[k]) for k in (2, 1, 3)]  13.9 us
    pallas_call x1, Pallas kernels, fit(): pl.pallas_call(functools.partial(fit_kernel, at), in_specs=[ON_SMEM, ON_V...  10.7 us
    pallas_call x1, Pallas kernels, panel_columns(): pl.pallas_call(functools.partial(panel_kernel, at), in_specs=[ON_SMEM, ON...  9.22 us
    ppermute x2, waiting for transfers between devices, body(): mirrors.append(along(first, 1)(handed))  5.34 us
  transfers between devices with their start and end apart: 15, of which 7 were waited for; matrix products, arithmetic and copies ran while one was open for 1% of the time, Pallas kernels for 2%

profile of v1, /device:TPU:0, one launch (start us, length us, event | category | flops | bytes accessed | tf_op | source)
XLA Modules:
  0.0 188.2 jit_solution(6303850389621937002)
XLA Ops:
  0.0 1.3 broadcast_in_dim.2
  1.3 41.3 %all_to_all.10.same = bf16[64,128,128]{2,1,0:T(8,128)(2,1)S(1)} all-to-all(bf16[64,128,128]{2,1,0:T(8,128)(2,1)S(1)} %broadcast_in_dim.2), channel_id=1, replica_groups=mesh['z'=4,'core'=2,'y'=4,'x'=4] {'z','y','x'}, dimensions={0} | all-to-all | bytes 4194304 | tf_op jit(solution)/shard_map/all_to_all | solution.py:79
  44.5 2.1 %prepare.1.table = s32[258]{0:T(512)} custom-call(s32[3]{0:T(128)} %pad_add_fusion.place, s32[16,5]{1,0:T(8,128)} %copy.7.lam, s32[16]{0:T(128)} %tile_count.1, s32[16,5]{1,0:T(8,128)} %copy.8.screen), custom_call_target="tpu_custom_call" | custom-call | tf_op jit(solution)/shard_map/prepare/pallas_call | solution.py:68
  47.5 10.7 %fit.1 = bf16[16,9,16,1024]{3,2,1,0:T(8,128)(2,1)S(1)} custom-call(s32[258]{0:T(512)S(1)} %copy-done, bf16[64,128,128]{2,1,0:T(8,128)(2,1)S(1)} %all_to_all.10.same, bf16[64,128,128]{2,1,0:T(8,128)(2,1)} %collective-permute-done.other, bf16[16,5,9,128,128]{4,3,2,1,0:T(8,128)(2,1)} %integrals.1), custom_call_target="tpu_custom_call" | custom-call | flops 3000000000 | bytes 20000000 | tf_op jit(solution)/shard_map/fit/pallas_call | solution.py:148
  58.2 60.7 %all_to_all.11.fitted = bf16[16,9,16,1024]{3,2,1,0:T(8,128)(2,1)S(1)} all-to-all(bf16[16,9,16,1024]{3,2,1,0:T(8,128)(2,1)S(1)} %fit.1), channel_id=1, replica_groups=mesh['z'=4,'core'=2,'y'=4,'x'=4] {'y','x'}, dimensions={0} | all-to-all | bytes 9437184 | tf_op jit(solution)/shard_map/all_to_all | solution.py:368
  118.9 3.4 %factor.1 = (bf16[1152,2048]{1,0:T(8,128)(2,1)S(1)}, bf16[2048,1152]{1,0:T(8,128)(2,1)S(1)}) custom-call(bf16[144,144]{1,0:T(8,128)(2,1)S(1)} %copy-done.1, bf16[16,9,16,1024]{3,2,1,0:T(8,128)(2,1)S(1)} %all_to_all.11.fitted), custom_call_target="tpu_custom_call" | custom-call | flops 2000000000 | bytes 10000000 | tf_op jit(solution)/shard_map/factor/pallas_call | solution.py:201
  122.3 9.2 %panel_columns.1 = (bf16[4,128,640]{2,1,0:T(8,128)(2,1)S(1)}, bf16[4,128,640]{2,1,0:T(8,128)(2,1)S(1)}, bf16[4,128,640]{2,1,0:T(8,128)(2,1)S(1)}, bf16[4,128,640...) custom-call(s32[258]{0:T(512)S(1)} %copy-done, ...), custom_call_target="tpu_custom_call" | custom-call | flops 8000000000 | bytes 15000000 | tf_op jit(solution)/shard_map/panel_columns/pallas_call | solution.py:252
  131.5 0.9 collective-permute-start.1
  132.5 0.9 collective-permute-start.2
  133.3 2.4 %collective-permute-start.3 = (bf16[4,128,640]{2,1,0:T(8,128)(2,1)S(1)}, bf16[4,128,640]{2,1,0:T(8,128)(2,1)S(1)}, u32[]{:S(2)}, u32[]{:S(2)}) collective-permute-start(bf16[4,128,640]{2,1,0:T(8,128)(2,1)S(1)} %get-tuple-element.32), channel_id=1, source_target_pairs={{0,12},{4,0},{8,4},{12,8},{1,13},{5,1},{9,5},{13,9},{2,14},{6,2},{... | collective-permute-start | bytes 1966088 | tf_op jit(solution)/shard_map/ppermute | solution.py:372
  135.7 1.2 collective-permute-start.7
  137.7 13.1 %collective-permute-done.1.rest_1_ = bf16[4,128,640]{2,1,0:T(8,128)(2,1)S(1)} collective-permute-done((bf16[4,128,640]{2,1,0:T(8,128)(2,1)S(1)}, bf16[4,128,640]{2,1,0:T(8,128)(2,1)S(1)}, u32[]{:S(2)}, u32[]{:S(2)}) %collective-permute-start.1) | collective-permute-done | bytes 655392 | tf_op jit(solution)/shard_map/ppermute | solution.py:372
  151.0 11.9 %collective-permute-done.2.rest_2_ = bf16[4,128,640]{2,1,0:T(8,128)(2,1)S(1)} collective-permute-done((bf16[4,128,640]{2,1,0:T(8,128)(2,1)S(1)}, bf16[4,128,640]{2,1,0:T(8,128)(2,1)S(1)}, u32[]{:S(2)}, u32[]{:S(2)}) %collective-permute-start.2) | collective-permute-done | bytes 655392 | tf_op jit(solution)/shard_map/ppermute | solution.py:372
  162.9 1.1 first_sum.2
  163.9 0.9 collective-permute-start.4
  164.9 3.2 %collective-permute-start.6 = (bf16[128,1024]{1,0:T(8,128)(2,1)S(1)}, bf16[128,1024]{1,0:T(8,128)(2,1)S(1)}, u32[]{:S(2)}, u32[]{:S(2)}) collective-permute-start(bf16[128,1024]{1,0:T(8,128)(2,1)S(1)} %get-tuple-element.36), channel_id=1, source_target_pairs={{0,3},{1,0},{2,1},{3,2},{4,7},{5,4},{6,5},{7,6},{8,11},{9,8},{10,9... | collective-permute-start | bytes 786440 | tf_op jit(solution)/shard_map/ppermute | solution.py:372
  168.1 0.9 first_sum.3
  169.1 1.6 collective-permute-start.10
  170.6 0.9 collective-permute-start.11
  171.6 3.2 %collective-permute-done.4.refs_1_ = bf16[128,1024]{1,0:T(8,128)(2,1)S(1)} collective-permute-done((bf16[128,1024]{1,0:T(8,128)(2,1)S(1)}, bf16[128,1024]{1,0:T(8,128)(2,1)S(1)}, u32[]{:S(2)}, u32[]{:S(2)}) %collective-permute-start.4) | collective-permute-done | bytes 262176 | tf_op jit(solution)/shard_map/ppermute | solution.py:372
  175.6 3.8 %collective-permute-done.5.refs_2_ = bf16[128,1024]{1,0:T(8,128)(2,1)S(1)} collective-permute-done((bf16[128,1024]{1,0:T(8,128)(2,1)S(1)}, bf16[128,1024]{1,0:T(8,128)(2,1)S(1)}, u32[]{:S(2)}, u32[]{:S(2)}) %collective-permute-start.5) | collective-permute-done | bytes 262176 | tf_op jit(solution)/shard_map/ppermute | solution.py:372
  179.7 1.1 collective-permute-done.11.refs_2_
  181.2 5.3 %collective-permute-done.14.rest_3_ = bf16[2,128,128]{2,1,0:T(8,128)(2,1)S(1)} collective-permute-done((bf16[2,128,128]{2,1,0:T(8,128)(2,1)S(1)}, bf16[2,128,128]{2,1,0:T(8,128)(2,1)S(1)}, u32[]{:S(2)}, u32[]{:S(2)}) %collective-permute-start.14) | collective-permute-done | bytes 65568 | tf_op jit(solution)/shard_map/ppermute | solution.py:381
  186.6 1.6 place_blocks.1
  (29 shorter events, 5.4 us)
Async XLA Ops:
  0.0 42.5 %copy-start.2 = (s32[16,5]{0,1:T(8,128)S(1)}, s32[16,5]{0,1:T(8,128)}, u32[]{:S(2)}) copy-start(s32[16,5]{0,1:T(8,128)} %param.7) | copy-start | bytes 964
  0.0 43.2 %copy-start.3 = (s32[16,5]{0,1:T(8,128)S(1)}, s32[16,5]{0,1:T(8,128)}, u32[]{:S(2)}) copy-start(s32[16,5]{0,1:T(8,128)} %param.9) | copy-start | bytes 964
  42.5 4.3 %collective-permute-start = (bf16[64,128,128]{2,1,0:T(8,128)(2,1)S(1)}, bf16[64,128,128]{2,1,0:T(8,128)(2,1)}, u32[]{:S(2)}, u32[]{:S(2)}) collective-permute-start(bf16[64,128,128]{2,1,0:T(8,128)(2,1)S(1)} %all_to_all.10.same), channel_id=1, source_target_pairs={{0,16},{16,0},{1,17},{17,1},{2,18},{18,2},{3,19},{19,3},{4,20},{20... | collective-permute-start | bytes 6291464 | tf_op jit(solution)/shard_map/ppermute | solution.py:80
  46.8 0.7 copy-start
  58.2 60.8 %copy-start.1 = (bf16[144,144]{1,0:T(8,128)(2,1)S(1)}, bf16[144,144]{1,0:T(8,128)(2,1)}, u32[]{:S(2)}) copy-start(bf16[144,144]{1,0:T(8,128)(2,1)} %metric.1) | copy-start | bytes 124420
  131.5 19.3 %collective-permute-start.1 = (bf16[4,128,640]{2,1,0:T(8,128)(2,1)S(1)}, bf16[4,128,640]{2,1,0:T(8,128)(2,1)S(1)}, u32[]{:S(2)}, u32[]{:S(2)}) collective-permute-start(bf16[4,128,640]{2,1,0:T(8,128)(2,1)S(1)} %get-tuple-element.30), channel_id=1, source_target_pairs={{0,8},{4,12},{8,0},{12,4},{1,9},{5,13},{9,1},{13,5},{2,10},{6,14},... | collective-permute-start | bytes 1966088 | tf_op jit(solution)/shard_map/ppermute | solution.py:372
  132.5 30.4 %collective-permute-start.2 = (bf16[4,128,640]{2,1,0:T(8,128)(2,1)S(1)}, bf16[4,128,640]{2,1,0:T(8,128)(2,1)S(1)}, u32[]{:S(2)}, u32[]{:S(2)}) collective-permute-start(bf16[4,128,640]{2,1,0:T(8,128)(2,1)S(1)} %get-tuple-element.31), channel_id=1, source_target_pairs={{0,4},{4,8},{8,12},{12,0},{1,5},{5,9},{9,13},{13,1},{2,6},{6,10},{... | collective-permute-start | bytes 1966088 | tf_op jit(solution)/shard_map/ppermute | solution.py:372
  133.3 29.6 %collective-permute-start.3 = (bf16[4,128,640]{2,1,0:T(8,128)(2,1)S(1)}, bf16[4,128,640]{2,1,0:T(8,128)(2,1)S(1)}, u32[]{:S(2)}, u32[]{:S(2)}) collective-permute-start(bf16[4,128,640]{2,1,0:T(8,128)(2,1)S(1)} %get-tuple-element.32), channel_id=1, source_target_pairs={{0,12},{4,0},{8,4},{12,8},{1,13},{5,1},{9,5},{13,9},{2,14},{6,2},{... | collective-permute-start | bytes 1966088 | tf_op jit(solution)/shard_map/ppermute | solution.py:372
  135.7 29.2 %collective-permute-start.7 = (bf16[4,128,640]{2,1,0:T(8,128)(2,1)S(1)}, bf16[4,128,640]{2,1,0:T(8,128)(2,1)S(1)}, u32[]{:S(2)}, u32[]{:S(2)}) collective-permute-start(bf16[4,128,640]{2,1,0:T(8,128)(2,1)S(1)} %get-tuple-element.39), channel_id=1, source_target_pairs={{0,2},{1,3},{2,0},{3,1},{4,6},{5,7},{6,4},{7,5},{8,10},{9,11},{10,... | collective-permute-start | bytes 1966088 | tf_op jit(solution)/shard_map/ppermute | solution.py:372
  136.9 31.2 %collective-permute-start.8 = (bf16[4,128,640]{2,1,0:T(8,128)(2,1)S(1)}, bf16[4,128,640]{2,1,0:T(8,128)(2,1)S(1)}, u32[]{:S(2)}, u32[]{:S(2)}) collective-permute-start(bf16[4,128,640]{2,1,0:T(8,128)(2,1)S(1)} %get-tuple-element.40), channel_id=1, source_target_pairs={{0,1},{1,2},{2,3},{3,0},{4,5},{5,6},{6,7},{7,4},{8,9},{9,10},{10,1... | collective-permute-start | bytes 1966088 | tf_op jit(solution)/shard_map/ppermute | solution.py:372
  150.8 17.3 %collective-permute-start.9 = (bf16[4,128,640]{2,1,0:T(8,128)(2,1)S(1)}, bf16[4,128,640]{2,1,0:T(8,128)(2,1)S(1)}, u32[]{:S(2)}, u32[]{:S(2)}) collective-permute-start(bf16[4,128,640]{2,1,0:T(8,128)(2,1)S(1)} %get-tuple-element.41), channel_id=1, source_target_pairs={{0,3},{1,0},{2,1},{3,2},{4,7},{5,4},{6,5},{7,6},{8,11},{9,8},{10,9... | collective-permute-start | bytes 1966088 | tf_op jit(solution)/shard_map/ppermute | solution.py:372
  163.9 10.8 %collective-permute-start.4 = (bf16[128,1024]{1,0:T(8,128)(2,1)S(1)}, bf16[128,1024]{1,0:T(8,128)(2,1)S(1)}, u32[]{:S(2)}, u32[]{:S(2)}) collective-permute-start(bf16[128,1024]{1,0:T(8,128)(2,1)S(1)} %get-tuple-element.34), channel_id=1, source_target_pairs={{0,2},{1,3},{2,0},{3,1},{4,6},{5,7},{6,4},{7,5},{8,10},{9,11},{10,... | collective-permute-start | bytes 786440 | tf_op jit(solution)/shard_map/ppermute | solution.py:372
  164.9 14.5 %collective-permute-start.5 = (bf16[128,1024]{1,0:T(8,128)(2,1)S(1)}, bf16[128,1024]{1,0:T(8,128)(2,1)S(1)}, u32[]{:S(2)}, u32[]{:S(2)}) collective-permute-start(bf16[128,1024]{1,0:T(8,128)(2,1)S(1)} %get-tuple-element.35), channel_id=1, source_target_pairs={{0,1},{1,2},{2,3},{3,0},{4,5},{5,6},{6,7},{7,4},{8,9},{9,10},{10,1... | collective-permute-start | bytes 786440 | tf_op jit(solution)/shard_map/ppermute | solution.py:372
  164.9 14.5 %collective-permute-start.6 = (bf16[128,1024]{1,0:T(8,128)(2,1)S(1)}, bf16[128,1024]{1,0:T(8,128)(2,1)S(1)}, u32[]{:S(2)}, u32[]{:S(2)}) collective-permute-start(bf16[128,1024]{1,0:T(8,128)(2,1)S(1)} %get-tuple-element.36), channel_id=1, source_target_pairs={{0,3},{1,0},{2,1},{3,2},{4,7},{5,4},{6,5},{7,6},{8,11},{9,8},{10,9... | collective-permute-start | bytes 786440 | tf_op jit(solution)/shard_map/ppermute | solution.py:372
  169.1 10.6 %collective-permute-start.10 = (bf16[128,768]{1,0:T(8,128)(2,1)S(1)}, bf16[128,768]{1,0:T(8,128)(2,1)S(1)}, u32[]{:S(2)}, u32[]{:S(2)}) collective-permute-start(bf16[128,768]{1,0:T(8,128)(2,1)S(1)} %get-tuple-element.43), channel_id=1, source_target_pairs={{0,8},{4,12},{8,0},{12,4},{1,9},{5,13},{9,1},{13,5},{2,10},{6,14},... | collective-permute-start | bytes 589832 | tf_op jit(solution)/shard_map/ppermute | solution.py:372
  170.6 10.2 %collective-permute-start.11 = (bf16[128,768]{1,0:T(8,128)(2,1)S(1)}, bf16[128,768]{1,0:T(8,128)(2,1)S(1)}, u32[]{:S(2)}, u32[]{:S(2)}) collective-permute-start(bf16[128,768]{1,0:T(8,128)(2,1)S(1)} %get-tuple-element.44), channel_id=1, source_target_pairs={{0,4},{4,8},{8,12},{12,0},{1,5},{5,9},{9,13},{13,1},{2,6},{6,10},{... | collective-permute-start | bytes 589832 | tf_op jit(solution)/shard_map/ppermute | solution.py:372
  174.7 6.1 %collective-permute-start.12 = (bf16[128,768]{1,0:T(8,128)(2,1)S(1)}, bf16[128,768]{1,0:T(8,128)(2,1)S(1)}, u32[]{:S(2)}, u32[]{:S(2)}) collective-permute-start(bf16[128,768]{1,0:T(8,128)(2,1)S(1)} %get-tuple-element.45), channel_id=1, source_target_pairs={{0,12},{4,0},{8,4},{12,8},{1,13},{5,1},{9,5},{13,9},{2,14},{6,2},{... | collective-permute-start | bytes 589832 | tf_op jit(solution)/shard_map/ppermute | solution.py:372
  179.6 6.9 %collective-permute-start.13 = (bf16[4,128,128]{2,1,0:T(8,128)(2,1)S(1)}, bf16[4,128,128]{2,1,0:T(8,128)(2,1)S(1)}, u32[]{:S(2)}, u32[]{:S(2)}) collective-permute-start(bf16[4,128,128]{2,1,0:T(8,128)(2,1)S(1)} %get-tuple-element.47), channel_id=1, source_target_pairs={{0,4},{4,8},{8,12},{12,0},{1,5},{5,9},{9,13},{13,1},{2,6},{6,10},{... | collective-permute-start | bytes 393224 | tf_op jit(solution)/shard_map/ppermute | solution.py:381
  181.0 5.5 %collective-permute-start.14 = (bf16[2,128,128]{2,1,0:T(8,128)(2,1)S(1)}, bf16[2,128,128]{2,1,0:T(8,128)(2,1)S(1)}, u32[]{:S(2)}, u32[]{:S(2)}) collective-permute-start(bf16[2,128,128]{2,1,0:T(8,128)(2,1)S(1)} %get-tuple-element.48), channel_id=1, source_target_pairs={{0,1},{1,2},{2,3},{3,0},{4,5},{5,6},{6,7},{7,4},{8,9},{9,10},{10,1... | collective-permute-start | bytes 196616 | tf_op jit(solution)/shard_map/ppermute | solution.py:381

commit v2 on v1

--- a/solution.py
+++ b/solution.py
@@ -51,12 +51,12 @@
     def one(b, _):
         count = jnp.int32(0)
         for s in range(at.slots):
-            name = lam[b, s]
+            name = lam[s, b]
             to = b * at.slots + count
             table[at.slot + to] = s
             table[at.core + to] = ((name >> 4) ^ core) & 1
             table[at.name + to] = ((name >> 5) << 4) | (name & 15)
-            keep = jnp.logical_and(s < tile_count[b], screen[b, s] > 0)
+            keep = jnp.logical_and(s < tile_count[b], screen[s, b] > 0)
             count = count + keep.astype(jnp.int32)
         table[at.count + b] = count
         return 0
@@ -71,7 +71,7 @@
         out_specs=ON_SMEM,
         out_shape=jax.ShapeDtypeStruct((at.size,), jnp.int32),
         name="prepare",
-    )(place, lam, tile_count, screen)
+    )(place, lam.T, tile_count, screen.T)
 
 
 def gather(coefficients):
@@ -83,9 +83,8 @@
 def fit_kernel(at, table, same, other, integrals, out, tiles, picked, total, done):
     slots = at.slots
     _, _, size = same.shape
-    ri, own_q, rows, _ = out.shape
+    ri, steps, own_q, rows, _ = out.shape
     share = rows // HALVES
-    steps = at.blocks // HALVES
 
     def copy(block, j):
         slot = table[at.slot + block * slots + j]
@@ -132,9 +131,7 @@
             parts = [
                 total[half, :, q * size:(q + 1) * size].reshape(ri, share, size) for half in range(HALVES)
             ]
-            out[:, q, :, pl.ds(pl.multiple_of(step * size, size), size)] = (
-                jnp.concatenate(parts, axis=1).astype(out.dtype)
-            )
+            out[:, step, q] = jnp.concatenate(parts, axis=1).astype(out.dtype)
         return 0
 
     lax.fori_loop(0, steps, one, 0)
@@ -155,7 +152,7 @@
             pltpu.VMEM((HALVES, occupied, own_q * size), jnp.float32),
             pltpu.SemaphoreType.DMA((blocks, slots)),
         ],
-        out_shape=jax.ShapeDtypeStruct((ri, own_q, HALVES * share, blocks // HALVES * size), jnp.bfloat16),
+        out_shape=jax.ShapeDtypeStruct((ri, blocks // HALVES, own_q, HALVES * share, size), jnp.bfloat16),
         compiler_params=pltpu.CompilerParams(vmem_limit_bytes=40 * MIB),
         cost_estimate=pl.CostEstimate(flops=3 * 10 ** 9, bytes_accessed=20 * 10 ** 6, transcendentals=0),
         name="fit",
@@ -163,21 +160,22 @@
 
 
 def factor_kernel(metric, fitted, factors, turned, wide):
-    ri, own_q, rows, half_cols = fitted.shape
+    ri, steps, own_q, rows, tile = fitted.shape
     share = rows // HALVES
     n_q = metric.shape[0]
-    lanes, tile = wide.shape[1], wide.shape[3]
+    lanes = wide.shape[1]
     chunk = lanes * tile
+    half_cols = steps * tile
 
     def one(c, _):
         base = pl.multiple_of(c * chunk, chunk)
         for k in range(own_q):
-            x = fitted[:, k, :, pl.ds(base, chunk)].astype(jnp.float32)
-            for r in range(ri):
-                to = (r * own_q + k) * share
-                for h in range(HALVES):
-                    for t in range(lanes):
-                        wide[h, t, to:to + share, :] = x[r, h * share:(h + 1) * share, t * tile:(t + 1) * tile]
+            for t in range(lanes):
+                x = fitted[:, c * lanes + t, k].astype(jnp.float32)
+                for r in range(ri):
+                    to = (r * own_q + k) * share
+                    for h in range(HALVES):
+                        wide[h, t, to:to + share, :] = x[r, h * share:(h + 1) * share]
         for h in range(HALVES):
             start = pl.multiple_of(base + h * half_cols, chunk)
             parts = []
@@ -191,12 +189,12 @@
             turned[pl.ds(start, chunk), :] = whole.T
         return 0
 
-    lax.fori_loop(0, half_cols // chunk, one, 0)
+    lax.fori_loop(0, steps // lanes, one, 0)
 
 
 def factor(metric, fitted):
-    ri, own_q, rows, half_cols = fitted.shape
-    cols = HALVES * half_cols
+    ri, steps, own_q, rows, size = fitted.shape
+    cols = HALVES * steps * size
     depth = own_q * ri * rows // HALVES
     return pl.pallas_call(
         factor_kernel,
@@ -206,7 +204,7 @@
             jax.ShapeDtypeStruct((depth, cols), jnp.bfloat16),
             jax.ShapeDtypeStruct((cols, depth), jnp.bfloat16),
         ],
-        scratch_shapes=[pltpu.VMEM((HALVES, 2, depth, cols // ri), jnp.float32)],
+        scratch_shapes=[pltpu.VMEM((HALVES, 2, depth, size), jnp.float32)],
         compiler_params=pltpu.CompilerParams(vmem_limit_bytes=20 * MIB),
         cost_estimate=pl.CostEstimate(flops=2 * 10 ** 9, bytes_accessed=10 * 10 ** 6, transcendentals=0),
         name="factor",

time: 189 us -> 188 us (level)
  transfers between devices with their start and end apart: 15 -> 15, of which waited for: 7 -> 7; matrix products, arithmetic and copies ran while one was open for 1% -> 0% of each run, Pallas kernels for 2% -> 2%
where the time goes in v2:
time: 188 us; the launch traced here: 187 us
  blocking collectives  101 us (54%)
  waiting for transfers between devices  40.4 us (21%)
  Pallas kernels  28.4 us (15%)
  starting transfers between devices  14.3 us (8%)
  local copies, waits for them, and re-layouts  1.94 us (1%)
    all_to_all x1, blocking collectives, body(): fitted = lax.all_to_all(mine, ('y', 'x'), 0, 0, tiled=True)  60.1 us
    all_to_all x1, blocking collectives, gather(): same = lax.all_to_all(copies, ('z', 'y', 'x'), 0, 0, tiled=True)  41.3 us
    ppermute x12, waiting for transfers between devices, send(): return [parts[0]] + [along(axis, k)(parts[k]) for k in (2, 1, 3)]  33.4 us
    ppermute x12, starting transfers between devices, send(): return [parts[0]] + [along(axis, k)(parts[k]) for k in (2, 1, 3)]  14.2 us
    pallas_call x1, Pallas kernels, fit(): pl.pallas_call(functools.partial(fit_kernel, at), in_specs=[ON_SMEM, ON_V...  9.85 us
    pallas_call x1, Pallas kernels, panel_columns(): pl.pallas_call(functools.partial(panel_kernel, at), in_specs=[ON_SMEM, ON...  9.21 us
    ppermute x2, waiting for transfers between devices, body(): mirrors.append(along(first, 1)(handed))  5.47 us
  transfers between devices with their start and end apart: 15, of which 7 were waited for; matrix products, arithmetic and copies ran while one was open for 0% of the time, Pallas kernels for 2%

profile of v2, /device:TPU:0, one launch (start us, length us, event | category | flops | bytes accessed | tf_op | source)
XLA Modules:
  0.0 187.2 jit_solution(15723599612043751668)
XLA Ops:
  0.0 1.2 broadcast_in_dim.2
  1.3 41.3 %all_to_all.10.same = bf16[64,128,128]{2,1,0:T(8,128)(2,1)S(1)} all-to-all(bf16[64,128,128]{2,1,0:T(8,128)(2,1)S(1)} %broadcast_in_dim.2), channel_id=1, replica_groups=mesh['z'=4,'core'=2,'y'=4,'x'=4] {'z','y','x'}, dimensions={0} | all-to-all | bytes 4194304 | tf_op jit(solution)/shard_map/all_to_all | solution.py:79
  43.2 2.0 %prepare.1.table = s32[258]{0:T(512)} custom-call(s32[3]{0:T(128)} %pad_add_fusion.place, s32[5,16]{1,0:T(8,128)} %bitcast.5, s32[16]{0:T(128)} %tile_count.1, s32[5,16]{1,0:T(8,128)} %bitcast.6), custom_call_target="tpu_custom_call" | custom-call | tf_op jit(solution)/shard_map/prepare/pallas_call | solution.py:68
  45.2 1.6 collective-permute-done.other
  47.5 9.8 %fit.1 = bf16[16,8,9,16,128]{4,3,2,1,0:T(8,128)(2,1)S(1)} custom-call(s32[258]{0:T(512)S(1)} %copy-done, bf16[64,128,128]{2,1,0:T(8,128)(2,1)S(1)} %all_to_all.10.same, bf16[64,128,128]{2,1,0:T(8,128)(2,1)} %collective-permute-done.other, bf16[16,5,9,128,128]{4,3,2,1,0:T(8,128)(2,1)} %integrals.1), custom_call_target="tpu_custom_call" | custom-call | flops 3000000000 | bytes 20000000 | tf_op jit(solution)/shard_map/fit/pallas_call | solution.py:145
  57.4 60.1 %all_to_all.11.fitted = bf16[16,8,9,16,128]{4,3,2,1,0:T(8,128)(2,1)S(1)} all-to-all(bf16[16,8,9,16,128]{4,3,2,1,0:T(8,128)(2,1)S(1)} %fit.1), channel_id=1, replica_groups=mesh['z'=4,'core'=2,'y'=4,'x'=4] {'y','x'}, dimensions={0} | all-to-all | bytes 9437184 | tf_op jit(solution)/shard_map/all_to_all | solution.py:366
  117.5 3.3 %factor.1 = (bf16[1152,2048]{1,0:T(8,128)(2,1)S(1)}, bf16[2048,1152]{1,0:T(8,128)(2,1)S(1)}) custom-call(bf16[144,144]{1,0:T(8,128)(2,1)S(1)} %copy-done.1, bf16[16,8,9,16,128]{4,3,2,1,0:T(8,128)(2,1)S(1)} %all_to_all.11.fitted), custom_call_target="tpu_custom_call" | custom-call | flops 2000000000 | bytes 10000000 | tf_op jit(solution)/shard_map/factor/pallas_call | solution.py:199
  120.7 9.2 %panel_columns.1 = (bf16[4,128,640]{2,1,0:T(8,128)(2,1)S(1)}, bf16[4,128,640]{2,1,0:T(8,128)(2,1)S(1)}, bf16[4,128,640]{2,1,0:T(8,128)(2,1)S(1)}, bf16[4,128,640...) custom-call(s32[258]{0:T(512)S(1)} %copy-done, ...), custom_call_target="tpu_custom_call" | custom-call | flops 8000000000 | bytes 15000000 | tf_op jit(solution)/shard_map/panel_columns/pallas_call | solution.py:250
  130.0 0.9 collective-permute-start.1
  130.9 0.9 collective-permute-start.2
  131.7 2.4 %collective-permute-start.3 = (bf16[4,128,640]{2,1,0:T(8,128)(2,1)S(1)}, bf16[4,128,640]{2,1,0:T(8,128)(2,1)S(1)}, u32[]{:S(2)}, u32[]{:S(2)}) collective-permute-start(bf16[4,128,640]{2,1,0:T(8,128)(2,1)S(1)} %get-tuple-element.32), channel_id=1, source_target_pairs={{0,12},{4,0},{8,4},{12,8},{1,13},{5,1},{9,5},{13,9},{2,14},{6,2},{... | collective-permute-start | bytes 1966088 | tf_op jit(solution)/shard_map/ppermute | solution.py:370
  134.1 1.5 collective-permute-start.7
  136.2 13.1 %collective-permute-done.1.rest_1_ = bf16[4,128,640]{2,1,0:T(8,128)(2,1)S(1)} collective-permute-done((bf16[4,128,640]{2,1,0:T(8,128)(2,1)S(1)}, bf16[4,128,640]{2,1,0:T(8,128)(2,1)S(1)}, u32[]{:S(2)}, u32[]{:S(2)}) %collective-permute-start.1) | collective-permute-done | bytes 655392 | tf_op jit(solution)/shard_map/ppermute | solution.py:370
  149.8 11.2 %collective-permute-done.2.rest_2_ = bf16[4,128,640]{2,1,0:T(8,128)(2,1)S(1)} collective-permute-done((bf16[4,128,640]{2,1,0:T(8,128)(2,1)S(1)}, bf16[4,128,640]{2,1,0:T(8,128)(2,1)S(1)}, u32[]{:S(2)}, u32[]{:S(2)}) %collective-permute-start.2) | collective-permute-done | bytes 655392 | tf_op jit(solution)/shard_map/ppermute | solution.py:370
  161.0 1.1 first_sum.2
  162.1 1.8 collective-permute-start.4
  163.9 3.2 %collective-permute-start.6 = (bf16[128,1024]{1,0:T(8,128)(2,1)S(1)}, bf16[128,1024]{1,0:T(8,128)(2,1)S(1)}, u32[]{:S(2)}, u32[]{:S(2)}) collective-permute-start(bf16[128,1024]{1,0:T(8,128)(2,1)S(1)} %get-tuple-element.36), channel_id=1, source_target_pairs={{0,3},{1,0},{2,1},{3,2},{4,7},{5,4},{6,5},{7,6},{8,11},{9,8},{10,9... | collective-permute-start | bytes 786440 | tf_op jit(solution)/shard_map/ppermute | solution.py:370
  167.1 0.9 first_sum.3
  168.1 1.2 collective-permute-start.10
  169.6 3.3 %collective-permute-done.4.refs_1_ = bf16[128,1024]{1,0:T(8,128)(2,1)S(1)} collective-permute-done((bf16[128,1024]{1,0:T(8,128)(2,1)S(1)}, bf16[128,1024]{1,0:T(8,128)(2,1)S(1)}, u32[]{:S(2)}, u32[]{:S(2)}) %collective-permute-start.4) | collective-permute-done | bytes 262176 | tf_op jit(solution)/shard_map/ppermute | solution.py:370
  173.7 3.8 %collective-permute-done.5.refs_2_ = bf16[128,1024]{1,0:T(8,128)(2,1)S(1)} collective-permute-done((bf16[128,1024]{1,0:T(8,128)(2,1)S(1)}, bf16[128,1024]{1,0:T(8,128)(2,1)S(1)}, u32[]{:S(2)}, u32[]{:S(2)}) %collective-permute-start.5) | collective-permute-done | bytes 262176 | tf_op jit(solution)/shard_map/ppermute | solution.py:370
  177.8 2.0 %collective-permute-done.11.refs_2_ = bf16[128,768]{1,0:T(8,128)(2,1)S(1)} collective-permute-done((bf16[128,768]{1,0:T(8,128)(2,1)S(1)}, bf16[128,768]{1,0:T(8,128)(2,1)S(1)}, u32[]{:S(2)}, u32[]{:S(2)}) %collective-permute-start.11) | collective-permute-done | bytes 196640 | tf_op jit(solution)/shard_map/ppermute | solution.py:370
  180.1 5.5 %collective-permute-done.14.rest_3_ = bf16[2,128,128]{2,1,0:T(8,128)(2,1)S(1)} collective-permute-done((bf16[2,128,128]{2,1,0:T(8,128)(2,1)S(1)}, bf16[2,128,128]{2,1,0:T(8,128)(2,1)S(1)}, u32[]{:S(2)}, u32[]{:S(2)}) %collective-permute-start.14) | collective-permute-done | bytes 65568 | tf_op jit(solution)/shard_map/ppermute | solution.py:379
  185.6 1.6 place_blocks.1
  (23 shorter events, 4.2 us)
Async XLA Ops:
  42.5 4.3 %collective-permute-start = (bf16[64,128,128]{2,1,0:T(8,128)(2,1)S(1)}, bf16[64,128,128]{2,1,0:T(8,128)(2,1)}, u32[]{:S(2)}, u32[]{:S(2)}) collective-permute-start(bf16[64,128,128]{2,1,0:T(8,128)(2,1)S(1)} %all_to_all.10.same), channel_id=1, source_target_pairs={{0,16},{16,0},{1,17},{17,1},{2,18},{18,2},{3,19},{19,3},{4,20},{20... | collective-permute-start | bytes 6291464 | tf_op jit(solution)/shard_map/ppermute | solution.py:80
  46.8 0.7 copy-start
  57.3 60.1 %copy-start.1 = (bf16[144,144]{1,0:T(8,128)(2,1)S(1)}, bf16[144,144]{1,0:T(8,128)(2,1)}, u32[]{:S(2)}) copy-start(bf16[144,144]{1,0:T(8,128)(2,1)} %metric.1) | copy-start | bytes 124420
  130.0 19.3 %collective-permute-start.1 = (bf16[4,128,640]{2,1,0:T(8,128)(2,1)S(1)}, bf16[4,128,640]{2,1,0:T(8,128)(2,1)S(1)}, u32[]{:S(2)}, u32[]{:S(2)}) collective-permute-start(bf16[4,128,640]{2,1,0:T(8,128)(2,1)S(1)} %get-tuple-element.30), channel_id=1, source_target_pairs={{0,8},{4,12},{8,0},{12,4},{1,9},{5,13},{9,1},{13,5},{2,10},{6,14},... | collective-permute-start | bytes 1966088 | tf_op jit(solution)/shard_map/ppermute | solution.py:370
  130.9 30.1 %collective-permute-start.2 = (bf16[4,128,640]{2,1,0:T(8,128)(2,1)S(1)}, bf16[4,128,640]{2,1,0:T(8,128)(2,1)S(1)}, u32[]{:S(2)}, u32[]{:S(2)}) collective-permute-start(bf16[4,128,640]{2,1,0:T(8,128)(2,1)S(1)} %get-tuple-element.31), channel_id=1, source_target_pairs={{0,4},{4,8},{8,12},{12,0},{1,5},{5,9},{9,13},{13,1},{2,6},{6,10},{... | collective-permute-start | bytes 1966088 | tf_op jit(solution)/shard_map/ppermute | solution.py:370
  131.7 29.3 %collective-permute-start.3 = (bf16[4,128,640]{2,1,0:T(8,128)(2,1)S(1)}, bf16[4,128,640]{2,1,0:T(8,128)(2,1)S(1)}, u32[]{:S(2)}, u32[]{:S(2)}) collective-permute-start(bf16[4,128,640]{2,1,0:T(8,128)(2,1)S(1)} %get-tuple-element.32), channel_id=1, source_target_pairs={{0,12},{4,0},{8,4},{12,8},{1,13},{5,1},{9,5},{13,9},{2,14},{6,2},{... | collective-permute-start | bytes 1966088 | tf_op jit(solution)/shard_map/ppermute | solution.py:370
  134.1 29.7 %collective-permute-start.7 = (bf16[4,128,640]{2,1,0:T(8,128)(2,1)S(1)}, bf16[4,128,640]{2,1,0:T(8,128)(2,1)S(1)}, u32[]{:S(2)}, u32[]{:S(2)}) collective-permute-start(bf16[4,128,640]{2,1,0:T(8,128)(2,1)S(1)} %get-tuple-element.39), channel_id=1, source_target_pairs={{0,2},{1,3},{2,0},{3,1},{4,6},{5,7},{6,4},{7,5},{8,10},{9,11},{10,... | collective-permute-start | bytes 1966088 | tf_op jit(solution)/shard_map/ppermute | solution.py:370
  135.6 31.5 %collective-permute-start.8 = (bf16[4,128,640]{2,1,0:T(8,128)(2,1)S(1)}, bf16[4,128,640]{2,1,0:T(8,128)(2,1)S(1)}, u32[]{:S(2)}, u32[]{:S(2)}) collective-permute-start(bf16[4,128,640]{2,1,0:T(8,128)(2,1)S(1)} %get-tuple-element.40), channel_id=1, source_target_pairs={{0,1},{1,2},{2,3},{3,0},{4,5},{5,6},{6,7},{7,4},{8,9},{9,10},{10,1... | collective-permute-start | bytes 1966088 | tf_op jit(solution)/shard_map/ppermute | solution.py:370
  149.2 17.9 %collective-permute-start.9 = (bf16[4,128,640]{2,1,0:T(8,128)(2,1)S(1)}, bf16[4,128,640]{2,1,0:T(8,128)(2,1)S(1)}, u32[]{:S(2)}, u32[]{:S(2)}) collective-permute-start(bf16[4,128,640]{2,1,0:T(8,128)(2,1)S(1)} %get-tuple-element.41), channel_id=1, source_target_pairs={{0,3},{1,0},{2,1},{3,2},{4,7},{5,4},{6,5},{7,6},{8,11},{9,8},{10,9... | collective-permute-start | bytes 1966088 | tf_op jit(solution)/shard_map/ppermute | solution.py:370
  162.1 10.8 %collective-permute-start.4 = (bf16[128,1024]{1,0:T(8,128)(2,1)S(1)}, bf16[128,1024]{1,0:T(8,128)(2,1)S(1)}, u32[]{:S(2)}, u32[]{:S(2)}) collective-permute-start(bf16[128,1024]{1,0:T(8,128)(2,1)S(1)} %get-tuple-element.34), channel_id=1, source_target_pairs={{0,2},{1,3},{2,0},{3,1},{4,6},{5,7},{6,4},{7,5},{8,10},{9,11},{10,... | collective-permute-start | bytes 786440 | tf_op jit(solution)/shard_map/ppermute | solution.py:370
  163.9 13.7 %collective-permute-start.5 = (bf16[128,1024]{1,0:T(8,128)(2,1)S(1)}, bf16[128,1024]{1,0:T(8,128)(2,1)S(1)}, u32[]{:S(2)}, u32[]{:S(2)}) collective-permute-start(bf16[128,1024]{1,0:T(8,128)(2,1)S(1)} %get-tuple-element.35), channel_id=1, source_target_pairs={{0,1},{1,2},{2,3},{3,0},{4,5},{5,6},{6,7},{7,4},{8,9},{9,10},{10,1... | collective-permute-start | bytes 786440 | tf_op jit(solution)/shard_map/ppermute | solution.py:370
  163.9 13.6 %collective-permute-start.6 = (bf16[128,1024]{1,0:T(8,128)(2,1)S(1)}, bf16[128,1024]{1,0:T(8,128)(2,1)S(1)}, u32[]{:S(2)}, u32[]{:S(2)}) collective-permute-start(bf16[128,1024]{1,0:T(8,128)(2,1)S(1)} %get-tuple-element.36), channel_id=1, source_target_pairs={{0,3},{1,0},{2,1},{3,2},{4,7},{5,4},{6,5},{7,6},{8,11},{9,8},{10,9... | collective-permute-start | bytes 786440 | tf_op jit(solution)/shard_map/ppermute | solution.py:370
  168.1 9.8 %collective-permute-start.10 = (bf16[128,768]{1,0:T(8,128)(2,1)S(1)}, bf16[128,768]{1,0:T(8,128)(2,1)S(1)}, u32[]{:S(2)}, u32[]{:S(2)}) collective-permute-start(bf16[128,768]{1,0:T(8,128)(2,1)S(1)} %get-tuple-element.43), channel_id=1, source_target_pairs={{0,8},{4,12},{8,0},{12,4},{1,9},{5,13},{9,1},{13,5},{2,10},{6,14},... | collective-permute-start | bytes 589832 | tf_op jit(solution)/shard_map/ppermute | solution.py:370
  169.3 10.5 %collective-permute-start.11 = (bf16[128,768]{1,0:T(8,128)(2,1)S(1)}, bf16[128,768]{1,0:T(8,128)(2,1)S(1)}, u32[]{:S(2)}, u32[]{:S(2)}) collective-permute-start(bf16[128,768]{1,0:T(8,128)(2,1)S(1)} %get-tuple-element.44), channel_id=1, source_target_pairs={{0,4},{4,8},{8,12},{12,0},{1,5},{5,9},{9,13},{13,1},{2,6},{6,10},{... | collective-permute-start | bytes 589832 | tf_op jit(solution)/shard_map/ppermute | solution.py:370
  172.9 7.0 %collective-permute-start.12 = (bf16[128,768]{1,0:T(8,128)(2,1)S(1)}, bf16[128,768]{1,0:T(8,128)(2,1)S(1)}, u32[]{:S(2)}, u32[]{:S(2)}) collective-permute-start(bf16[128,768]{1,0:T(8,128)(2,1)S(1)} %get-tuple-element.45), channel_id=1, source_target_pairs={{0,12},{4,0},{8,4},{12,8},{1,13},{5,1},{9,5},{13,9},{2,14},{6,2},{... | collective-permute-start | bytes 589832 | tf_op jit(solution)/shard_map/ppermute | solution.py:370
  177.8 7.8 %collective-permute-start.13 = (bf16[4,128,128]{2,1,0:T(8,128)(2,1)S(1)}, bf16[4,128,128]{2,1,0:T(8,128)(2,1)S(1)}, u32[]{:S(2)}, u32[]{:S(2)}) collective-permute-start(bf16[4,128,128]{2,1,0:T(8,128)(2,1)S(1)} %get-tuple-element.47), channel_id=1, source_target_pairs={{0,4},{4,8},{8,12},{12,0},{1,5},{5,9},{9,13},{13,1},{2,6},{6,10},{... | collective-permute-start | bytes 393224 | tf_op jit(solution)/shard_map/ppermute | solution.py:379
  180.0 5.5 %collective-permute-start.14 = (bf16[2,128,128]{2,1,0:T(8,128)(2,1)S(1)}, bf16[2,128,128]{2,1,0:T(8,128)(2,1)S(1)}, u32[]{:S(2)}, u32[]{:S(2)}) collective-permute-start(bf16[2,128,128]{2,1,0:T(8,128)(2,1)S(1)} %get-tuple-element.48), channel_id=1, source_target_pairs={{0,1},{1,2},{2,3},{3,0},{4,5},{5,6},{6,7},{7,4},{8,9},{9,10},{10,1... | collective-permute-start | bytes 196616 | tf_op jit(solution)/shard_map/ppermute | solution.py:379

commit v3 on v2

--- a/solution.py
+++ b/solution.py
@@ -80,7 +80,7 @@
     return same, lax.ppermute(same, "core", [(0, 1), (1, 0)])
 
 
-def fit_kernel(at, table, same, other, integrals, out, tiles, picked, total, done):
+def fit_kernel(at, table, same, other_core, integrals, out, tiles, others, picked, total, done, arrived):
     slots = at.slots
     _, _, size = same.shape
     ri, steps, own_q, rows, _ = out.shape
@@ -101,7 +101,10 @@
             kept(step + half * steps, lambda c: c.start())
         return 0
 
+    swap = pltpu.make_async_copy(other_core, others, arrived)
+    swap.start()
     lax.fori_loop(0, steps, begin, 0)
+    swap.wait()
 
     def one(step, _):
         for half in range(HALVES):
@@ -119,7 +122,7 @@
                     for j in range(c):
                         n = block * slots + j
                         name = table[at.name + n]
-                        tile = jnp.where(table[at.core + n] == 0, same[name], other[name])
+                        tile = jnp.where(table[at.core + n] == 0, same[name], others[name])
                         picked[half, :, j * size:(j + 1) * size] = tile
                     wide = [tiles[block, j].reshape(own_q * size, size) for j in range(c)]
                     wide = jnp.concatenate(wide, axis=1) if c > 1 else wide[0]
@@ -144,13 +147,15 @@
     share = occupied // ri
     return pl.pallas_call(
         functools.partial(fit_kernel, at),
-        in_specs=[ON_SMEM, ON_VMEM, ON_VMEM, ANYWHERE],
+        in_specs=[ON_SMEM, ON_VMEM, ANYWHERE, ANYWHERE],
         out_specs=ON_VMEM,
         scratch_shapes=[
             pltpu.VMEM((blocks, slots, own_q, size, size), jnp.bfloat16),
+            pltpu.VMEM(other.shape, jnp.bfloat16),
             pltpu.VMEM((HALVES, occupied, slots * size), jnp.bfloat16),
             pltpu.VMEM((HALVES, occupied, own_q * size), jnp.float32),
             pltpu.SemaphoreType.DMA((blocks, slots)),
+            pltpu.SemaphoreType.DMA,
         ],
         out_shape=jax.ShapeDtypeStruct((ri, blocks // HALVES, own_q, HALVES * share, size), jnp.bfloat16),
         compiler_params=pltpu.CompilerParams(vmem_limit_bytes=40 * MIB),

time: 188 us -> 188 us (level)
  no operation moved by 1% of the time
where the time goes in v3:
time: 188 us
  blocking collectives  102 us (54%)
  waiting for transfers between devices  40.7 us (22%)
  Pallas kernels  27.8 us (15%)
  starting transfers between devices  14 us (7%)
  local copies, waits for them, and re-layouts  1.94 us (1%)
    all_to_all x1, blocking collectives, body(): fitted = lax.all_to_all(mine, ('y', 'x'), 0, 0, tiled=True)  61.1 us
    all_to_all x1, blocking collectives, gather(): same = lax.all_to_all(copies, ('z', 'y', 'x'), 0, 0, tiled=True)  41.3 us
    ppermute x12, waiting for transfers between devices, send(): return [parts[0]] + [along(axis, k)(parts[k]) for k in (2, 1, 3)]  33.7 us
    ppermute x12, starting transfers between devices, send(): return [parts[0]] + [along(axis, k)(parts[k]) for k in (2, 1, 3)]  13.9 us
    pallas_call x1, Pallas kernels, panel_columns(): pl.pallas_call(functools.partial(panel_kernel, at), in_specs=[ON_SMEM, ON...  9.22 us
    pallas_call x1, Pallas kernels, fit(): pl.pallas_call(functools.partial(fit_kernel, at), in_specs=[ON_SMEM, ON_V...  9.21 us
    ppermute x2, waiting for transfers between devices, body(): mirrors.append(along(first, 1)(handed))  5.47 us
  transfers between devices with their start and end apart: 15, of which 7 were waited for; matrix products, arithmetic and copies ran while one was open for 0% of the time, Pallas kernels for 2%

profile of v3, /device:TPU:0, one launch (start us, length us, event | category | flops | bytes accessed | tf_op | source)
XLA Modules:
  0.0 187.6 jit_solution(8891190023762902397)
XLA Ops:
  0.0 1.2 broadcast_in_dim.2
  1.3 41.3 %all_to_all.10.same = bf16[64,128,128]{2,1,0:T(8,128)(2,1)S(1)} all-to-all(bf16[64,128,128]{2,1,0:T(8,128)(2,1)S(1)} %broadcast_in_dim.2), channel_id=1, replica_groups=mesh['z'=4,'core'=2,'y'=4,'x'=4] {'z','y','x'}, dimensions={0} | all-to-all | bytes 4194304 | tf_op jit(solution)/shard_map/all_to_all | solution.py:79
  43.2 2.0 %prepare.1.table = s32[258]{0:T(512)} custom-call(s32[3]{0:T(128)} %pad_add_fusion.place, s32[5,16]{1,0:T(8,128)} %bitcast.5, s32[16]{0:T(128)} %tile_count.1, s32[5,16]{1,0:T(8,128)} %bitcast.6), custom_call_target="tpu_custom_call" | custom-call | tf_op jit(solution)/shard_map/prepare/pallas_call | solution.py:68
  45.2 1.6 collective-permute-done.other_core
  47.5 9.2 %fit.1 = bf16[16,8,9,16,128]{4,3,2,1,0:T(8,128)(2,1)S(1)} custom-call(s32[258]{0:T(512)S(1)} %copy-done, bf16[64,128,128]{2,1,0:T(8,128)(2,1)S(1)} %all_to_all.10.same, bf16[64,128,128]{2,1,0:T(8,128)(2,1)} %collective-permute-done.other_core, bf16[16,5,9,128,128]{4,3,2,1,0:T(8,128)(2,1)} %integrals.1), custom_call_target="tpu_custom_call" | custom-call | flops 3000000000 | bytes 20000000 | tf_op jit(solution)/shard_map/fit/pallas_call | solution.py:148
  56.7 61.1 %all_to_all.11.fitted = bf16[16,8,9,16,128]{4,3,2,1,0:T(8,128)(2,1)S(1)} all-to-all(bf16[16,8,9,16,128]{4,3,2,1,0:T(8,128)(2,1)S(1)} %fit.1), channel_id=1, replica_groups=mesh['z'=4,'core'=2,'y'=4,'x'=4] {'y','x'}, dimensions={0} | all-to-all | bytes 9437184 | tf_op jit(solution)/shard_map/all_to_all | solution.py:371
  117.8 3.3 %factor.1 = (bf16[1152,2048]{1,0:T(8,128)(2,1)S(1)}, bf16[2048,1152]{1,0:T(8,128)(2,1)S(1)}) custom-call(bf16[144,144]{1,0:T(8,128)(2,1)S(1)} %copy-done.1, bf16[16,8,9,16,128]{4,3,2,1,0:T(8,128)(2,1)S(1)} %all_to_all.11.fitted), custom_call_target="tpu_custom_call" | custom-call | flops 2000000000 | bytes 10000000 | tf_op jit(solution)/shard_map/factor/pallas_call | solution.py:204
  121.0 9.2 %panel_columns.1 = (bf16[4,128,640]{2,1,0:T(8,128)(2,1)S(1)}, bf16[4,128,640]{2,1,0:T(8,128)(2,1)S(1)}, bf16[4,128,640]{2,1,0:T(8,128)(2,1)S(1)}, bf16[4,128,640...) custom-call(s32[258]{0:T(512)S(1)} %copy-done, ...), custom_call_target="tpu_custom_call" | custom-call | flops 8000000000 | bytes 15000000 | tf_op jit(solution)/shard_map/panel_columns/pallas_call | solution.py:255
  130.3 0.9 collective-permute-start.1
  131.2 0.9 collective-permute-start.2
  132.1 2.4 %collective-permute-start.3 = (bf16[4,128,640]{2,1,0:T(8,128)(2,1)S(1)}, bf16[4,128,640]{2,1,0:T(8,128)(2,1)S(1)}, u32[]{:S(2)}, u32[]{:S(2)}) collective-permute-start(bf16[4,128,640]{2,1,0:T(8,128)(2,1)S(1)} %get-tuple-element.32), channel_id=1, source_target_pairs={{0,12},{4,0},{8,4},{12,8},{1,13},{5,1},{9,5},{13,9},{2,14},{6,2},{... | collective-permute-start | bytes 1966088 | tf_op jit(solution)/shard_map/ppermute | solution.py:375
  134.4 1.6 collective-permute-start.7
  136.5 13.1 %collective-permute-done.1.rest_1_ = bf16[4,128,640]{2,1,0:T(8,128)(2,1)S(1)} collective-permute-done((bf16[4,128,640]{2,1,0:T(8,128)(2,1)S(1)}, bf16[4,128,640]{2,1,0:T(8,128)(2,1)S(1)}, u32[]{:S(2)}, u32[]{:S(2)}) %collective-permute-start.1) | collective-permute-done | bytes 655392 | tf_op jit(solution)/shard_map/ppermute | solution.py:375
  149.7 12.2 %collective-permute-done.2.rest_2_ = bf16[4,128,640]{2,1,0:T(8,128)(2,1)S(1)} collective-permute-done((bf16[4,128,640]{2,1,0:T(8,128)(2,1)S(1)}, bf16[4,128,640]{2,1,0:T(8,128)(2,1)S(1)}, u32[]{:S(2)}, u32[]{:S(2)}) %collective-permute-start.2) | collective-permute-done | bytes 655392 | tf_op jit(solution)/shard_map/ppermute | solution.py:375
  162.0 1.1 first_sum.2
  163.0 1.2 collective-permute-start.4
  164.2 3.2 %collective-permute-start.6 = (bf16[128,1024]{1,0:T(8,128)(2,1)S(1)}, bf16[128,1024]{1,0:T(8,128)(2,1)S(1)}, u32[]{:S(2)}, u32[]{:S(2)}) collective-permute-start(bf16[128,1024]{1,0:T(8,128)(2,1)S(1)} %get-tuple-element.36), channel_id=1, source_target_pairs={{0,3},{1,0},{2,1},{3,2},{4,7},{5,4},{6,5},{7,6},{8,11},{9,8},{10,9... | collective-permute-start | bytes 786440 | tf_op jit(solution)/shard_map/ppermute | solution.py:375
  167.5 0.9 first_sum.3
  168.4 1.7 collective-permute-start.10
  170.7 3.1 %collective-permute-done.4.refs_1_ = bf16[128,1024]{1,0:T(8,128)(2,1)S(1)} collective-permute-done((bf16[128,1024]{1,0:T(8,128)(2,1)S(1)}, bf16[128,1024]{1,0:T(8,128)(2,1)S(1)}, u32[]{:S(2)}, u32[]{:S(2)}) %collective-permute-start.4) | collective-permute-done | bytes 262176 | tf_op jit(solution)/shard_map/ppermute | solution.py:375
  174.7 3.8 %collective-permute-done.5.refs_2_ = bf16[128,1024]{1,0:T(8,128)(2,1)S(1)} collective-permute-done((bf16[128,1024]{1,0:T(8,128)(2,1)S(1)}, bf16[128,1024]{1,0:T(8,128)(2,1)S(1)}, u32[]{:S(2)}, u32[]{:S(2)}) %collective-permute-start.5) | collective-permute-done | bytes 262176 | tf_op jit(solution)/shard_map/ppermute | solution.py:375
  178.8 1.4 collective-permute-done.11.refs_2_
  180.5 5.5 %collective-permute-done.14.rest_3_ = bf16[2,128,128]{2,1,0:T(8,128)(2,1)S(1)} collective-permute-done((bf16[2,128,128]{2,1,0:T(8,128)(2,1)S(1)}, bf16[2,128,128]{2,1,0:T(8,128)(2,1)S(1)}, u32[]{:S(2)}, u32[]{:S(2)}) %collective-permute-start.14) | collective-permute-done | bytes 65568 | tf_op jit(solution)/shard_map/ppermute | solution.py:384
  185.9 1.6 place_blocks.1
  (23 shorter events, 3.9 us)
Async XLA Ops:
  42.5 4.3 %collective-permute-start = (bf16[64,128,128]{2,1,0:T(8,128)(2,1)S(1)}, bf16[64,128,128]{2,1,0:T(8,128)(2,1)}, u32[]{:S(2)}, u32[]{:S(2)}) collective-permute-start(bf16[64,128,128]{2,1,0:T(8,128)(2,1)S(1)} %all_to_all.10.same), channel_id=1, source_target_pairs={{0,16},{16,0},{1,17},{17,1},{2,18},{18,2},{3,19},{19,3},{4,20},{20... | collective-permute-start | bytes 6291464 | tf_op jit(solution)/shard_map/ppermute | solution.py:80
  46.8 0.7 copy-start
  56.7 61.1 %copy-start.1 = (bf16[144,144]{1,0:T(8,128)(2,1)S(1)}, bf16[144,144]{1,0:T(8,128)(2,1)}, u32[]{:S(2)}) copy-start(bf16[144,144]{1,0:T(8,128)(2,1)} %metric.1) | copy-start | bytes 124420
  130.3 19.3 %collective-permute-start.1 = (bf16[4,128,640]{2,1,0:T(8,128)(2,1)S(1)}, bf16[4,128,640]{2,1,0:T(8,128)(2,1)S(1)}, u32[]{:S(2)}, u32[]{:S(2)}) collective-permute-start(bf16[4,128,640]{2,1,0:T(8,128)(2,1)S(1)} %get-tuple-element.30), channel_id=1, source_target_pairs={{0,8},{4,12},{8,0},{12,4},{1,9},{5,13},{9,1},{13,5},{2,10},{6,14},... | collective-permute-start | bytes 1966088 | tf_op jit(solution)/shard_map/ppermute | solution.py:375
  131.2 30.8 %collective-permute-start.2 = (bf16[4,128,640]{2,1,0:T(8,128)(2,1)S(1)}, bf16[4,128,640]{2,1,0:T(8,128)(2,1)S(1)}, u32[]{:S(2)}, u32[]{:S(2)}) collective-permute-start(bf16[4,128,640]{2,1,0:T(8,128)(2,1)S(1)} %get-tuple-element.31), channel_id=1, source_target_pairs={{0,4},{4,8},{8,12},{12,0},{1,5},{5,9},{9,13},{13,1},{2,6},{6,10},{... | collective-permute-start | bytes 1966088 | tf_op jit(solution)/shard_map/ppermute | solution.py:375
  132.1 29.9 %collective-permute-start.3 = (bf16[4,128,640]{2,1,0:T(8,128)(2,1)S(1)}, bf16[4,128,640]{2,1,0:T(8,128)(2,1)S(1)}, u32[]{:S(2)}, u32[]{:S(2)}) collective-permute-start(bf16[4,128,640]{2,1,0:T(8,128)(2,1)S(1)} %get-tuple-element.32), channel_id=1, source_target_pairs={{0,12},{4,0},{8,4},{12,8},{1,13},{5,1},{9,5},{13,9},{2,14},{6,2},{... | collective-permute-start | bytes 1966088 | tf_op jit(solution)/shard_map/ppermute | solution.py:375
  134.4 29.8 %collective-permute-start.7 = (bf16[4,128,640]{2,1,0:T(8,128)(2,1)S(1)}, bf16[4,128,640]{2,1,0:T(8,128)(2,1)S(1)}, u32[]{:S(2)}, u32[]{:S(2)}) collective-permute-start(bf16[4,128,640]{2,1,0:T(8,128)(2,1)S(1)} %get-tuple-element.39), channel_id=1, source_target_pairs={{0,2},{1,3},{2,0},{3,1},{4,6},{5,7},{6,4},{7,5},{8,10},{9,11},{10,... | collective-permute-start | bytes 1966088 | tf_op jit(solution)/shard_map/ppermute | solution.py:375
  136.0 31.4 %collective-permute-start.8 = (bf16[4,128,640]{2,1,0:T(8,128)(2,1)S(1)}, bf16[4,128,640]{2,1,0:T(8,128)(2,1)S(1)}, u32[]{:S(2)}, u32[]{:S(2)}) collective-permute-start(bf16[4,128,640]{2,1,0:T(8,128)(2,1)S(1)} %get-tuple-element.40), channel_id=1, source_target_pairs={{0,1},{1,2},{2,3},{3,0},{4,5},{5,6},{6,7},{7,4},{8,9},{9,10},{10,1... | collective-permute-start | bytes 1966088 | tf_op jit(solution)/shard_map/ppermute | solution.py:375
  149.6 17.9 %collective-permute-start.9 = (bf16[4,128,640]{2,1,0:T(8,128)(2,1)S(1)}, bf16[4,128,640]{2,1,0:T(8,128)(2,1)S(1)}, u32[]{:S(2)}, u32[]{:S(2)}) collective-permute-start(bf16[4,128,640]{2,1,0:T(8,128)(2,1)S(1)} %get-tuple-element.41), channel_id=1, source_target_pairs={{0,3},{1,0},{2,1},{3,2},{4,7},{5,4},{6,5},{7,6},{8,11},{9,8},{10,9... | collective-permute-start | bytes 1966088 | tf_op jit(solution)/shard_map/ppermute | solution.py:375
  163.0 10.8 %collective-permute-start.4 = (bf16[128,1024]{1,0:T(8,128)(2,1)S(1)}, bf16[128,1024]{1,0:T(8,128)(2,1)S(1)}, u32[]{:S(2)}, u32[]{:S(2)}) collective-permute-start(bf16[128,1024]{1,0:T(8,128)(2,1)S(1)} %get-tuple-element.34), channel_id=1, source_target_pairs={{0,2},{1,3},{2,0},{3,1},{4,6},{5,7},{6,4},{7,5},{8,10},{9,11},{10,... | collective-permute-start | bytes 786440 | tf_op jit(solution)/shard_map/ppermute | solution.py:375
  164.2 14.2 %collective-permute-start.5 = (bf16[128,1024]{1,0:T(8,128)(2,1)S(1)}, bf16[128,1024]{1,0:T(8,128)(2,1)S(1)}, u32[]{:S(2)}, u32[]{:S(2)}) collective-permute-start(bf16[128,1024]{1,0:T(8,128)(2,1)S(1)} %get-tuple-element.35), channel_id=1, source_target_pairs={{0,1},{1,2},{2,3},{3,0},{4,5},{5,6},{6,7},{7,4},{8,9},{9,10},{10,1... | collective-permute-start | bytes 786440 | tf_op jit(solution)/shard_map/ppermute | solution.py:375
  164.2 14.2 %collective-permute-start.6 = (bf16[128,1024]{1,0:T(8,128)(2,1)S(1)}, bf16[128,1024]{1,0:T(8,128)(2,1)S(1)}, u32[]{:S(2)}, u32[]{:S(2)}) collective-permute-start(bf16[128,1024]{1,0:T(8,128)(2,1)S(1)} %get-tuple-element.36), channel_id=1, source_target_pairs={{0,3},{1,0},{2,1},{3,2},{4,7},{5,4},{6,5},{7,6},{8,11},{9,8},{10,9... | collective-permute-start | bytes 786440 | tf_op jit(solution)/shard_map/ppermute | solution.py:375
  168.4 10.4 %collective-permute-start.10 = (bf16[128,768]{1,0:T(8,128)(2,1)S(1)}, bf16[128,768]{1,0:T(8,128)(2,1)S(1)}, u32[]{:S(2)}, u32[]{:S(2)}) collective-permute-start(bf16[128,768]{1,0:T(8,128)(2,1)S(1)} %get-tuple-element.43), channel_id=1, source_target_pairs={{0,8},{4,12},{8,0},{12,4},{1,9},{5,13},{9,1},{13,5},{2,10},{6,14},... | collective-permute-start | bytes 589832 | tf_op jit(solution)/shard_map/ppermute | solution.py:375
  170.2 10.0 %collective-permute-start.11 = (bf16[128,768]{1,0:T(8,128)(2,1)S(1)}, bf16[128,768]{1,0:T(8,128)(2,1)S(1)}, u32[]{:S(2)}, u32[]{:S(2)}) collective-permute-start(bf16[128,768]{1,0:T(8,128)(2,1)S(1)} %get-tuple-element.44), channel_id=1, source_target_pairs={{0,4},{4,8},{8,12},{12,0},{1,5},{5,9},{9,13},{13,1},{2,6},{6,10},{... | collective-permute-start | bytes 589832 | tf_op jit(solution)/shard_map/ppermute | solution.py:375
  173.8 6.4 %collective-permute-start.12 = (bf16[128,768]{1,0:T(8,128)(2,1)S(1)}, bf16[128,768]{1,0:T(8,128)(2,1)S(1)}, u32[]{:S(2)}, u32[]{:S(2)}) collective-permute-start(bf16[128,768]{1,0:T(8,128)(2,1)S(1)} %get-tuple-element.45), channel_id=1, source_target_pairs={{0,12},{4,0},{8,4},{12,8},{1,13},{5,1},{9,5},{13,9},{2,14},{6,2},{... | collective-permute-start | bytes 589832 | tf_op jit(solution)/shard_map/ppermute | solution.py:375
  178.7 7.2 %collective-permute-start.13 = (bf16[4,128,128]{2,1,0:T(8,128)(2,1)S(1)}, bf16[4,128,128]{2,1,0:T(8,128)(2,1)S(1)}, u32[]{:S(2)}, u32[]{:S(2)}) collective-permute-start(bf16[4,128,128]{2,1,0:T(8,128)(2,1)S(1)} %get-tuple-element.47), channel_id=1, source_target_pairs={{0,4},{4,8},{8,12},{12,0},{1,5},{5,9},{9,13},{13,1},{2,6},{6,10},{... | collective-permute-start | bytes 393224 | tf_op jit(solution)/shard_map/ppermute | solution.py:384
  180.4 5.5 %collective-permute-start.14 = (bf16[2,128,128]{2,1,0:T(8,128)(2,1)S(1)}, bf16[2,128,128]{2,1,0:T(8,128)(2,1)S(1)}, u32[]{:S(2)}, u32[]{:S(2)}) collective-permute-start(bf16[2,128,128]{2,1,0:T(8,128)(2,1)S(1)} %get-tuple-element.48), channel_id=1, source_target_pairs={{0,1},{1,2},{2,3},{3,0},{4,5},{5,6},{6,7},{7,4},{8,9},{9,10},{10,1... | collective-permute-start | bytes 196616 | tf_op jit(solution)/shard_map/ppermute | solution.py:384
